TPU v7x, 128 devices: a whole 4x4x4 slice. The times are simulated.
128 devices in a mesh: node: 4 (over x), expert: 32 (over z, y, core).
Axes of the slice: x: 4, y: 4, z: 4, core: 2. Of those that a mesh axis runs over, the one named last changes fastest.
Arguments:
- grad_out: bfloat16 [4096, 7168], P(('node', 'expert')), may hold values from -6 to 6
- logits: float32 [4096, 128], P(('node', 'expert')), may hold values from -6 to 6
- routes: int32 [4096, 8], P(('node', 'expert')), may hold values from 0 to 127, as said below
- w_down: bfloat16 [128, 1024, 7168], P(('node', 'expert')), may hold values from -0.1875 to 0.1875
- saved_hidden: bfloat16 [128, 512, 1024], P(('node', 'expert')), may hold values from -4 to 4
Outputs:
- d_hidden: bfloat16 [128, 512, 1024], P(('node', 'expert'))
- d_logits: float32 [4096, 128], P(('node', 'expert'))
Inputs may be any that keep to these rules, and one draw needn't show every extreme that they name: `routes`: each row names 8 different experts, four in each of two node groups (expert e lies in group e // 32); one group, drawn from the seed, is named by every row. Among the 32 rows of one device no expert is named by more than 4 rows, and each expert of that group by exactly 4.
All inputs are finite; a program needn't handle non-finite values.
Results may differ from a plain program's by a relative error of at most 0.0049.
Values may be sent and summed in bfloat16 or wider, within the bound.
No kernel may reach another device: no remote copies, remote signals or barrier semaphores. Data moves between devices by JAX's collectives and lax.ppermute only.
A program may use at most 128 MiB of HBM per device.

v0:
```python
import jax
import jax.numpy as jnp
from jax import lax
from jax.sharding import PartitionSpec as P

route_scale = 2.5


def pack_slots(grad_out, weights, slot_index, slot_total):
    spread = jnp.broadcast_to(
        grad_out[:, None, :], (grad_out.shape[0], slot_index.shape[1], grad_out.shape[1])
    )
    send_rows = jnp.zeros((slot_total, grad_out.shape[1]), jnp.bfloat16).at[slot_index].set(spread)
    send_weights = jnp.zeros((slot_total,), jnp.bfloat16).at[slot_index].set(weights)
    return (send_rows, send_weights)


def shards(grad_out, logits, routes, w_down, saved_hidden):
    feat_width = grad_out.shape[1]
    expert_count = logits.shape[1]
    capacity = saved_hidden.shape[1]
    slot_most = capacity // expert_count
    expert_ids = jnp.arange(expert_count, dtype=jnp.int32)
    picked = (routes[:, :, None] == expert_ids).astype(jnp.int32)
    routed = jnp.sum(picked, 1)
    earlier = jnp.cumsum(routed, 0) - routed
    position = jnp.take_along_axis(earlier, routes, 1)
    slot_index = routes * slot_most + position
    affinity = jax.nn.sigmoid(logits)
    chosen = jnp.take_along_axis(affinity, routes, 1)
    total = jnp.sum(chosen, 1, keepdims=True)
    weights = (route_scale * chosen / total).astype(jnp.bfloat16)
    send_rows, send_weights = pack_slots(grad_out, weights, slot_index, expert_count * slot_most)
    arrived, arrived_weights = (
        lax.all_to_all(
            send_rows.reshape(expert_count, slot_most, feat_width),
            ("node", "expert"),
            split_axis=0,
            concat_axis=0,
            tiled=True,
        ),
        lax.all_to_all(
            send_weights.reshape(expert_count, slot_most),
            ("node", "expert"),
            split_axis=0,
            concat_axis=0,
            tiled=True,
        ),
    )
    rows = arrived.reshape(capacity, feat_width)
    slot_weight = arrived_weights.reshape(capacity).astype(jnp.float32)
    raw = lax.dot_general(
        rows, w_down[0], (((1,), (1,)), ((), ())), preferred_element_type=jnp.float32
    )
    d_hidden = (slot_weight[:, None] * raw).astype(jnp.bfloat16)[None]
    route_grad = jnp.sum(raw * saved_hidden[0].astype(jnp.float32), 1)
    returned = lax.all_to_all(
        route_grad.reshape(expert_count, slot_most),
        ("node", "expert"),
        split_axis=0,
        concat_axis=0,
        tiled=True,
    )
    per_route = returned.reshape(-1)[slot_index]
    mean_grad = jnp.sum(per_route * chosen, 1, keepdims=True) / total
    d_chosen = route_scale / total * (per_route - mean_grad)
    d_affinity = d_chosen * chosen * (1.0 - chosen)
    d_logits = jnp.sum(picked.astype(jnp.float32) * d_affinity[:, :, None], 1)
    return (d_hidden, d_logits)


def solution(mesh):
    return jax.shard_map(
        shards,
        mesh=mesh,
        in_specs=(
            P(("node", "expert"), None),
            P(("node", "expert"), None),
            P(("node", "expert"), None),
            P(("node", "expert"), None, None),
            P(("node", "expert"), None, None),
        ),
        out_specs=(P(("node", "expert"), None, None), P(("node", "expert"), None)),
        check_vma=False,
    )
```

profile of v0, /device:TPU:1, one launch (start us, length us, event | category | flops | bytes accessed | tf_op | source)
XLA Modules:
  0.0 194.6 jit_solution(12689316388013310495)
XLA Ops:
  0.6 0.0 copy-start
  0.6 0.8 copy.21
  1.5 0.1 convert_reduce_fusion
  1.6 0.1 reduce_window_sum.11
  1.7 0.1 reshape.92
  1.7 1.9 gather_fusion.1
  3.7 0.1 reshape.95
  3.8 0.1 reshape.106
  3.8 0.0 copy-done
  3.9 9.6 %scatter_custom_fusion.1 = bf16[512,7168]{1,0:T(8,128)(2,1)} fusion(s32[256]{0:T(256)S(1)} %reshape.106, bf16[]{:T(256)} %constant.15.clone.1, bf16[32,7168]{1,0:T(8,128)(2,1)S(1)} %copy-done), kind=kCustom, calls=%fused_computation.7 | custom fusion | bytes 7798786 | tf_op jit(solution)/shard_map/scatter | solution.py:13
  13.4 12.6 %reshape.79 = bf16[128,4,7168]{2,1,0:T(4,128)(2,1)} reshape(bf16[512,7168]{1,0:T(8,128)(2,1)} %scatter_custom_fusion.1) | data formatting | bytes 14680064 | tf_op jit(solution)/shard_map/reshape | solution.py:36
  26.1 0.0 copy-start.1
  26.1 11.9 %all-to-all-start.1 = ((bf16[128,4,7168]{2,1,0:T(4,128)(2,1)}), bf16[128,4,7168]{2,1,0:T(4,128)(2,1)}, u32[]{:S(2)}, u32[]{:S(2)}) async-start(bf16[128,4,7168]{2,1,0:T(4,128)(2,1)} %reshape.79), calls=%async_computation.1 | async-start | bytes 14680064 | tf_op jit(solution)/shard_map/all_to_all | solution.py:35
  38.0 0.0 copy-done.1
  38.0 92.9 %all-to-all-done.1 = bf16[128,4,7168]{2,1,0:T(4,128)(2,1)} async-done(((bf16[128,4,7168]{2,1,0:T(4,128)(2,1)}), bf16[128,4,7168]{2,1,0:T(4,128)(2,1)}, u32[]{:S(2)}, u32[]{:S(2)}) %all-to-all-start.1) | async-done | bytes 7340064 | tf_op jit(solution)/shard_map/all_to_all | solution.py:35
  130.9 12.1 %reshape.80 = bf16[512,7168]{1,0:T(8,128)(2,1)} reshape(bf16[128,4,7168]{2,1,0:T(4,128)(2,1)} %all-to-all-done.1) | data formatting | bytes 14680064 | tf_op jit(solution)/shard_map/reshape | solution.py:50
  143.0 13.5 %fusion.5 = (f32[512]{0:T(512)S(1)}, f32[512,1024]{1,0:T(8,128)S(1)}) fusion(bf16[1,512,1024]{2,1,0:T(8,128)(2,1)} %param.9, bf16[512,7168]{1,0:T(8,128)(2,1)} %reshape.80, bf16[1,1024,7168]{2,1,0:T(8,128)(2,1)} %param.8), kind=kOutput, calls=%fused_computation.11 | convolution fusion | flops 7517765120 | bytes 25167872 | tf_op jit(solution)/shard_map/dot_general | solution.py:52
  156.5 0.7 all_to_all.18
  157.2 5.7 %all-to-all-start.2 = ((f32[128,1,4]{2,1,0:T(1,128)}), f32[128,1,4]{2,1,0:T(1,128)S(1)}, u32[]{:S(2)}, u32[]{:S(2)}) async-start(f32[128,1,4]{2,1,0:T(1,128)} %bitcast.5), calls=%async_computation.2 | async-start | bytes 131072 | tf_op jit(solution)/shard_map/all_to_all | solution.py:57
  163.0 1.9 gather_fusion.2
  164.9 0.1 reshape.101
  165.0 7.4 %all-to-all-done.2 = f32[128,1,4]{2,1,0:T(1,128)S(1)} async-done(((f32[128,1,4]{2,1,0:T(1,128)}), f32[128,1,4]{2,1,0:T(1,128)S(1)}, u32[]{:S(2)}, u32[]{:S(2)}) %all-to-all-start.2) | async-done | bytes 2080 | tf_op jit(solution)/shard_map/all_to_all | solution.py:57
  172.4 0.5 broadcast.81
  172.9 0.8 reduce.7
  173.7 0.1 reshape.81
  173.8 1.9 %gather_fusion = f32[256]{0:T(256)S(1)} fusion(f32[512]{0:T(512)S(1)} %reshape.81, s32[1024]{0:T(1024)S(1)} %pad_clamp_fusion), kind=kCustom, calls=%fused_computation | custom fusion | bytes 3072 | tf_op jit(solution)/shard_map/gather | solution.py:64
  175.8 0.1 reshape.85
  175.9 0.1 multiply_reduce_fusion
  176.0 0.1 subtract_multiply_fusion
  176.1 0.1 reshape.108
  176.2 2.2 %scatter_custom_fusion = bf16[512]{0:T(512)(128)(2,1)S(1)} fusion(s32[256]{0:T(256)S(1)} %reshape.106, bf16[256]{0:T(256)(128)(2,1)S(1)} %reshape.108, bf16[]{:T(256)} %constant.15.clone.1), kind=kCustom, calls=%fused_computation.32 | custom fusion | bytes 1026 | tf_op jit(solution)/shard_map/scatter | solution.py:14
  178.4 0.8 all_to_all.20
  179.1 4.6 %all-to-all-start = ((bf16[128,1,4]{2,1,0:T(2,128)(2,1)}), bf16[128,1,4]{2,1,0:T(2,128)(2,1)S(1)}, u32[]{:S(2)}, u32[]{:S(2)}) async-start(bf16[128,1,4]{2,1,0:T(2,128)(2,1)} %all_to_all.20), calls=%async_computation | async-start | bytes 131072 | tf_op jit(solution)/shard_map/all_to_all | solution.py:42
  183.7 0.7 fusion.9
  184.5 8.7 %all-to-all-done = bf16[128,1,4]{2,1,0:T(2,128)(2,1)S(1)} async-done(((bf16[128,1,4]{2,1,0:T(2,128)(2,1)}), bf16[128,1,4]{2,1,0:T(2,128)(2,1)S(1)}, u32[]{:S(2)}, u32[]{:S(2)}) %all-to-all-start) | async-done | bytes 1056 | tf_op jit(solution)/shard_map/all_to_all | solution.py:42
  193.2 0.2 convert_reduce_fusion.1
  193.4 0.1 reshape.82
  193.5 1.2 fusion.7
  (6 shorter events, 0.1 us)
Async XLA Ops:
  0.6 3.2 %copy-start = (bf16[32,7168]{1,0:T(8,128)(2,1)S(1)}, bf16[32,7168]{1,0:T(8,128)(2,1)}, u32[]{:S(2)}) copy-start(bf16[32,7168]{1,0:T(8,128)(2,1)} %param.5) | copy-start | bytes 1376260
  26.1 11.9 %copy-start.1 = (f32[32,128]{1,0:T(8,128)S(1)}, f32[32,128]{1,0:T(8,128)}, u32[]{:S(2)}) copy-start(f32[32,128]{1,0:T(8,128)} %param.6) | copy-start | bytes 49156
  26.1 104.9 %all-to-all-start.1 = ((bf16[128,4,7168]{2,1,0:T(4,128)(2,1)}), bf16[128,4,7168]{2,1,0:T(4,128)(2,1)}, u32[]{:S(2)}, u32[]{:S(2)}) async-start(bf16[128,4,7168]{2,1,0:T(4,128)(2,1)} %reshape.79), calls=%async_computation.1 | async-start | bytes 14680064 | tf_op jit(solution)/shard_map/all_to_all | solution.py:35
  157.2 15.1 %all-to-all-start.2 = ((f32[128,1,4]{2,1,0:T(1,128)}), f32[128,1,4]{2,1,0:T(1,128)S(1)}, u32[]{:S(2)}, u32[]{:S(2)}) async-start(f32[128,1,4]{2,1,0:T(1,128)} %bitcast.5), calls=%async_computation.2 | async-start | bytes 131072 | tf_op jit(solution)/shard_map/all_to_all | solution.py:57
  179.1 14.0 %all-to-all-start = ((bf16[128,1,4]{2,1,0:T(2,128)(2,1)}), bf16[128,1,4]{2,1,0:T(2,128)(2,1)S(1)}, u32[]{:S(2)}, u32[]{:S(2)}) async-start(bf16[128,1,4]{2,1,0:T(2,128)(2,1)} %all_to_all.20), calls=%async_computation | async-start | bytes 131072 | tf_op jit(solution)/shard_map/all_to_all | solution.py:42
where the time goes:
time: 195 us
  waiting for transfers between devices  109 us (56%)
  local copies, waits for them, and re-layouts  45.7 us (23%)
  starting transfers between devices  22.2 us (11%)
  matrix products  13.5 us (7%)
  other arithmetic  3.33 us (2%)
    all_to_all x1, waiting for transfers between devices, shards(): lax.all_to_all(send_rows.reshape(expert_count, slot_most, feat_width), ('...  92.9 us
    dot_general x1, matrix products, shards(): lax.dot_general(rows, w_down[0], (((1,), (1,)), ((), ())), preferred_elem...  13.5 us
    reshape x1, local copies, waits for them, and re-layouts, shards(): send_rows.reshape(expert_count, slot_most, feat_width)  12.6 us
    reshape x1, local copies, waits for them, and re-layouts, shards(): rows = arrived.reshape(capacity, feat_width)  12.1 us
    all_to_all x1, starting transfers between devices, shards(): lax.all_to_all(send_rows.reshape(expert_count, slot_most, feat_width), ('...  11.9 us
    scatter x1, local copies, waits for them, and re-layouts, pack_slots(): jnp.zeros((slot_total, grad_out.shape[1]), jnp.bfloat16).at[slot_index]  9.56 us
    all_to_all x1, waiting for transfers between devices, shards(): lax.all_to_all(send_weights.reshape(expert_count, slot_most), ('node', 'e...  8.67 us
    all_to_all x1, waiting for transfers between devices, shards(): lax.all_to_all(route_grad.reshape(expert_count, slot_most), ('node', 'exp...  7.42 us
  transfers between devices with their start and end apart: 3, of which 3 were waited for; matrix products, arithmetic and copies ran while one was open for 1% of the time, Pallas kernels for 0%

commit v1 on v0

v1 whole, which is shorter than its diff:
```python
import functools

import jax
import jax.numpy as jnp
from jax import lax
from jax.experimental import pallas as pl
from jax.experimental.pallas import tpu as pltpu
from jax.sharding import PartitionSpec as P

route_scale = 2.5
QUARTERS = 4
PIECE = 256
MIB = 1 << 20


def iota(shape, dim):
    return lax.broadcasted_iota(jnp.int32, shape, dim)


def slot_ranks(routes_t, experts):
    most, tokens = routes_t.shape
    ids = iota((experts, tokens), 0)
    picked = jnp.zeros((experts, tokens), jnp.float32)
    for k in range(most):
        picked += (routes_t[k : k + 1, :] == ids).astype(jnp.float32)
    before = (iota((tokens, tokens), 0) < iota((tokens, tokens), 1)).astype(jnp.bfloat16)
    earlier = jnp.dot(picked.astype(jnp.bfloat16), before, preferred_element_type=jnp.float32)
    return picked * (earlier + 1.0)


def pack_kernel(slots, routes_ref, grad_ref, out_ref, ranks, pieces):
    tokens, width = grad_ref.shape
    experts = ranks.shape[0]
    span = QUARTERS * PIECE

    @pl.when(pl.program_id(0) == 0)
    def _():
        found = slot_ranks(routes_ref[...], experts).astype(jnp.bfloat16)
        ranks[...] = jnp.concatenate([found] * QUARTERS, 1)
        for step in range(width // span):
            for q in range(QUARTERS):
                pieces[q * tokens : (q + 1) * tokens, step * PIECE : (step + 1) * PIECE] = grad_ref[
                    :, step * span + q * PIECE : step * span + (q + 1) * PIECE
                ]

    rows, columns = out_ref.shape[0], QUARTERS * tokens
    unit = QUARTERS * slots
    row = iota((rows, experts), 0) + pl.program_id(0) * rows
    spread = (row // unit == iota((rows, experts), 1)).astype(jnp.bfloat16)
    rank = jnp.dot(spread, ranks[...], preferred_element_type=jnp.float32)
    row = iota((rows, columns), 0)
    slot = (row % slots + 1).astype(jnp.float32)
    same = (row // slots) % QUARTERS == iota((rows, columns), 1) // tokens
    take = jnp.where(same & (rank == slot), 1.0, 0.0).astype(jnp.bfloat16)
    out_ref[...] = jnp.dot(take, pieces[...], preferred_element_type=jnp.float32).astype(jnp.bfloat16)


def weight_kernel(slots, routes_ref, logits_ref, out_ref, rank_ref, chosen_ref):
    tokens, experts = logits_ref.shape
    found = slot_ranks(routes_ref[...], experts).astype(jnp.bfloat16)
    unit = (iota((experts, experts), 0) == iota((experts, experts), 1)).astype(jnp.bfloat16)
    rank = lax.dot_general(found, unit, (((0,), (0,)), ((), ())), preferred_element_type=jnp.float32)
    rank_ref[...] = rank
    chosen = jnp.where(rank > 0.0, jax.nn.sigmoid(logits_ref[...]), 0.0)
    chosen_ref[...] = chosen
    total = jnp.sum(chosen, 1, keepdims=True)
    weights = (route_scale * chosen / total).astype(jnp.bfloat16).astype(jnp.float32)
    out = jnp.zeros((experts, experts), jnp.float32)
    lane = iota((tokens, experts), 1)
    for j in range(slots):
        mine = jnp.where(rank == j + 1.0, weights, 0.0).astype(jnp.bfloat16)
        to = (lane == slots + j).astype(jnp.bfloat16)
        out += lax.dot_general(mine, to, (((0,), (0,)), ((), ())), preferred_element_type=jnp.float32)
    out_ref[...] = out


def expert_kernel(slots, rows_ref, w_ref, hidden_ref, weights_ref, raw_ref, back_ref, rows):
    unit = QUARTERS * slots
    step = pl.program_id(0)
    block = 256
    each = block // QUARTERS
    to, came = iota((block, block), 0), iota((block, block), 1)
    source = (to % each) // slots * unit + to // each * slots + to % slots
    order = (came == source).astype(jnp.bfloat16)
    for b in range(rows_ref.shape[0] // block):
        turned = jnp.dot(
            order, rows_ref[b * block : (b + 1) * block, :], preferred_element_type=jnp.float32
        ).astype(jnp.bfloat16)
        for q in range(QUARTERS):
            rows[b * each : (b + 1) * each, q * PIECE : (q + 1) * PIECE] = turned[q * each : (q + 1) * each]
    part = lax.dot_general(
        rows[...], w_ref[...], (((1,), (1,)), ((), ())), preferred_element_type=jnp.float32
    )

    @pl.when(step == 0)
    def _():
        raw_ref[...] = part

    @pl.when(step > 0)
    def _():
        raw_ref[...] += part

    @pl.when(step == pl.num_programs(0) - 1)
    def _():
        capacity = raw_ref.shape[0]
        peers, lanes = back_ref.shape
        grads = jnp.sum(raw_ref[...] * hidden_ref[...].astype(jnp.float32), 1, keepdims=True)
        slot = iota((capacity, lanes), 0) % slots
        spread = jnp.where(slot == iota((capacity, lanes), 1), grads, 0.0)
        gather = (iota((peers, capacity), 0) == iota((peers, capacity), 1) // slots).astype(jnp.float32)
        back_ref[...] = weights_ref[...] + jnp.dot(
            gather, spread, preferred_element_type=jnp.float32, precision=lax.Precision.HIGHEST
        )


def final_kernel(slots, raw_ref, back_ref, rank_ref, chosen_ref, hidden_ref, logits_ref):
    block = raw_ref.shape[0]
    peers = block // slots
    lanes = back_ref.shape[1]
    start = pl.multiple_of(pl.program_id(0) * peers, peers)
    mine = back_ref[pl.ds(start, peers), :].astype(jnp.bfloat16)
    spread = (iota((block, peers), 0) // slots == iota((block, peers), 1)).astype(jnp.bfloat16)
    weight = jnp.dot(spread, mine, preferred_element_type=jnp.float32)
    slot = iota((block, lanes), 0) % slots
    weight = jnp.sum(jnp.where(slot + slots == iota((block, lanes), 1), weight, 0.0), 1, keepdims=True)
    hidden_ref[...] = (weight * raw_ref[...]).astype(jnp.bfloat16)

    @pl.when(pl.program_id(0) == 0)
    def _():
        rank = rank_ref[...]
        chosen = chosen_ref[...]
        total = jnp.sum(chosen, 1, keepdims=True)
        back = jnp.transpose(back_ref[...])
        per_route = jnp.zeros_like(chosen)
        for j in range(slots):
            per_route += jnp.where(rank == j + 1.0, back[j : j + 1, :], 0.0)
        mean_grad = jnp.sum(per_route * chosen, 1, keepdims=True) / total
        d_chosen = (route_scale / total) * (per_route - mean_grad)
        logits_ref[...] = jnp.where(rank > 0.0, d_chosen * chosen * (1.0 - chosen), 0.0)


def whole(shape):
    return pl.BlockSpec(shape, lambda i: (0,) * len(shape))


def params():
    return pltpu.CompilerParams(vmem_limit_bytes=40 * MIB)


def shards(grad_out, logits, routes, w_down, saved_hidden):
    tokens, width = grad_out.shape
    experts = logits.shape[1]
    capacity, units = saved_hidden.shape[1:]
    slots = capacity // experts
    unit = QUARTERS * slots
    narrow = width // QUARTERS
    routes_t = routes.T
    pack_rows = 256
    sent = pl.pallas_call(
        functools.partial(pack_kernel, slots),
        grid=(experts * unit // pack_rows,),
        in_specs=[whole(routes_t.shape), whole(grad_out.shape)],
        out_specs=pl.BlockSpec((pack_rows, narrow), lambda i: (i, 0)),
        out_shape=jax.ShapeDtypeStruct((experts * unit, narrow), jnp.bfloat16),
        scratch_shapes=[
            pltpu.VMEM((experts, QUARTERS * tokens), jnp.bfloat16),
            pltpu.VMEM((QUARTERS * tokens, narrow), jnp.bfloat16),
        ],
        compiler_params=params(),
        cost_estimate=pl.CostEstimate(
            flops=2 * experts * unit * narrow * QUARTERS * tokens,
            bytes_accessed=2 * experts * unit * narrow,
            transcendentals=0,
        ),
        name="pack",
    )(routes_t, grad_out)
    arrived = lax.all_to_all(
        sent.reshape(experts, unit, narrow), ("node", "expert"), split_axis=0, concat_axis=0, tiled=True
    ).reshape(experts * unit, narrow)
    weights, rank, chosen = pl.pallas_call(
        functools.partial(weight_kernel, slots),
        out_shape=(
            jax.ShapeDtypeStruct((experts, experts), jnp.float32),
            jax.ShapeDtypeStruct((tokens, experts), jnp.float32),
            jax.ShapeDtypeStruct((tokens, experts), jnp.float32),
        ),
        compiler_params=params(),
        name="weights",
    )(routes_t, logits)
    span = QUARTERS * PIECE
    raw, back = pl.pallas_call(
        functools.partial(expert_kernel, slots),
        grid=(width // span,),
        in_specs=[
            pl.BlockSpec((experts * unit, PIECE), lambda i: (0, i)),
            pl.BlockSpec((None, units, span), lambda i: (0, 0, i)),
            pl.BlockSpec((None, capacity, units), lambda i: (0, 0, 0)),
            whole((experts, experts)),
        ],
        out_specs=(whole((capacity, units)), whole((experts, experts))),
        out_shape=(
            jax.ShapeDtypeStruct((capacity, units), jnp.float32),
            jax.ShapeDtypeStruct((experts, experts), jnp.float32),
        ),
        scratch_shapes=[pltpu.VMEM((capacity, span), jnp.bfloat16)],
        compiler_params=params(),
        cost_estimate=pl.CostEstimate(
            flops=2 * capacity * units * width,
            bytes_accessed=2 * (units + capacity) * width + 4 * capacity * units,
            transcendentals=0,
        ),
        name="expert",
    )(arrived, w_down, saved_hidden, weights)
    returned = lax.all_to_all(
        back.reshape(experts, 1, experts), ("node", "expert"), split_axis=0, concat_axis=0, tiled=True
    ).reshape(experts, experts)
    final_rows = capacity // 4
    d_hidden, d_logits = pl.pallas_call(
        functools.partial(final_kernel, slots),
        grid=(4,),
        in_specs=[
            pl.BlockSpec((final_rows, units), lambda i: (i, 0)),
            whole((experts, experts)),
            whole((tokens, experts)),
            whole((tokens, experts)),
        ],
        out_specs=(
            pl.BlockSpec((None, final_rows, units), lambda i: (0, i, 0)),
            whole((tokens, experts)),
        ),
        out_shape=(
            jax.ShapeDtypeStruct((1, capacity, units), jnp.bfloat16),
            jax.ShapeDtypeStruct((tokens, experts), jnp.float32),
        ),
        compiler_params=params(),
        name="final",
    )(raw, returned, rank, chosen)
    return (d_hidden, d_logits)


def solution(mesh):
    return jax.shard_map(
        shards,
        mesh=mesh,
        in_specs=(
            P(("node", "expert"), None),
            P(("node", "expert"), None),
            P(("node", "expert"), None),
            P(("node", "expert"), None, None),
            P(("node", "expert"), None, None),
        ),
        out_specs=(P(("node", "expert"), None, None), P(("node", "expert"), None)),
        check_vma=False,
    )
```

time: 195 us -> 147 us (0.75)
  local copies, waits for them, and re-layouts: 45.7 us -> 4.71 us
  Pallas kernels: 0 us -> 22.8 us
  waiting for transfers between devices: 109 us -> 92 us
  blocking collectives: 0 us -> 14.7 us
  matrix products: 13.5 us -> 0 us
  starting transfers between devices: 22.2 us -> 11.9 us
  other arithmetic: 3.33 us -> 0 us
    reshape x3 -> x0, local copies, waits for them, and re-layouts: 24.8 us -> none  [the longest x1 12.6 us: shards(): send_rows.reshape(expert_count, slot_most, feat_width)]
    pallas_call x0 -> x4, Pallas kernels: none -> 22.8 us  [the longest x1 15.2 us: shards(): pl.pallas_call(functools.partial(expert_kernel, slots), grid=(width // sp...]
    all_to_all x3 -> x1, waiting for transfers between devices: 109 us -> 92 us  [shards(): lax.all_to_all(sent.reshape(experts, unit, narrow), ('node', 'expert'), s...]
    all_to_all x0 -> x1, blocking collectives: none -> 14.7 us  [shards(): lax.all_to_all(back.reshape(experts, 1, experts), ('node', 'expert'), spl...]
    dot_general x1 -> x0, matrix products: 13.5 us -> none  [shards(): lax.dot_general(rows, w_down[0], (((1,), (1,)), ((), ())), preferred_elem...]
    scatter x2 -> x0, local copies, waits for them, and re-layouts: 11.7 us -> none  [the longest x1 9.56 us: pack_slots(): jnp.zeros((slot_total, grad_out.shape[1]), jnp.bfloat16).at[slot_index]]
    all_to_all x3 -> x1, starting transfers between devices: 22.2 us -> 11.9 us  [shards(): lax.all_to_all(sent.reshape(experts, unit, narrow), ('node', 'expert'), s...]
    gather x7 -> x0, local copies, waits for them, and re-layouts: 6.07 us -> none  [the longest x3 2.06 us: shards(): position = jnp.take_along_axis(earlier, routes, 1)]
  transfers between devices with their start and end apart: 3 -> 1, of which waited for: 3 -> 1; matrix products, arithmetic and copies ran while one was open for 1% -> 0% of each run, Pallas kernels for 0% -> 0%
where the time goes in v1:
time: 147 us
  waiting for transfers between devices  92 us (63%)
  Pallas kernels  22.8 us (16%)
  blocking collectives  14.7 us (10%)
  starting transfers between devices  11.9 us (8%)
  local copies, waits for them, and re-layouts  4.71 us (3%)
    all_to_all x1, waiting for transfers between devices, shards(): lax.all_to_all(sent.reshape(experts, unit, narrow), ('node', 'expert'), s...  92 us
    pallas_call x1, Pallas kernels, shards(): pl.pallas_call(functools.partial(expert_kernel, slots), grid=(width // sp...  15.2 us
    all_to_all x1, blocking collectives, shards(): lax.all_to_all(back.reshape(experts, 1, experts), ('node', 'expert'), spl...  14.7 us
    all_to_all x1, starting transfers between devices, shards(): lax.all_to_all(sent.reshape(experts, unit, narrow), ('node', 'expert'), s...  11.9 us
    unnamed x12, local copies, waits for them, and re-layouts  4.71 us
    pallas_call x1, Pallas kernels, shards(): pl.pallas_call(functools.partial(pack_kernel, slots), grid=(experts * uni...  4.63 us
  transfers between devices with their start and end apart: 1, of which 1 were waited for; matrix products, arithmetic and copies ran while one was open for 0% of the time, Pallas kernels for 0%

profile of v1, /device:TPU:1, one launch (start us, length us, event | category | flops | bytes accessed | tf_op | source)
XLA Modules:
  0.0 146.7 jit_solution(9554414415477527931)
XLA Ops:
  0.6 0.0 copy-start.1
  0.6 1.0 copy-done.1
  1.6 0.0 copy-start.2
  1.7 0.7 copy-done.2
  2.3 4.6 %pack.1 = bf16[2048,1792]{1,0:T(8,128)(2,1)S(1)} custom-call(s32[8,32]{1,0:T(8,128)S(1)} %bitcast.10, bf16[32,7168]{1,0:T(8,128)(2,1)S(1)} %copy-done.1), custom_call_target="tpu_custom_call" | custom-call | flops 939524096 | bytes 7340032 | tf_op jit(solution)/shard_map/pack/pallas_call | solution.py:159
  7.0 0.0 copy-start
  7.0 3.0 %copy-done = bf16[2048,1792]{1,0:T(8,128)(2,1)} copy-done((bf16[2048,1792]{1,0:T(8,128)(2,1)}, bf16[2048,1792]{1,0:T(8,128)(2,1)S(1)}, u32[]{:S(2)}) %copy-start) | copy-done | bytes 7340056
  10.0 0.0 copy-start.3
  10.0 0.0 copy-start.4
  10.0 0.0 copy-start.5
  10.0 11.9 %all-to-all-start = ((bf16[128,16,1792]{2,1,0:T(8,128)(2,1)}), bf16[128,16,1792]{2,1,0:T(8,128)(2,1)}, u32[]{:S(2)}, u32[]{:S(2)}) async-start(bf16[128,16,1792]{2,1,0:T(8,128)(2,1)} %bitcast.7), calls=%async_computation | async-start | bytes 14680064 | tf_op jit(solution)/shard_map/all_to_all | solution.py:177
  21.9 0.0 copy-done.3
  21.9 0.0 copy-done.4
  21.9 0.6 weights.1
  22.6 92.0 %all-to-all-done = bf16[128,16,1792]{2,1,0:T(8,128)(2,1)} async-done(((bf16[128,16,1792]{2,1,0:T(8,128)(2,1)}), bf16[128,16,1792]{2,1,0:T(8,128)(2,1)}, u32[]{:S(2)}, u32[]{:S(2)}) %all-to-all-start) | async-done | bytes 7340064 | tf_op jit(solution)/shard_map/all_to_all | solution.py:177
  114.5 0.0 copy-done.5
  114.5 15.2 %expert.1 = (f32[512,1024]{1,0:T(8,128)S(1)}, f32[128,128]{1,0:T(8,128)S(1)}) custom-call(bf16[2048,1792]{1,0:T(8,128)(2,1)} %bitcast.2.rows_ref, bf16[1,1024,7168]{2,1,0:T(8,128)(2,1)} %w_ref.1, bf16[1,512,1024]{2,1,0:T(8,128)(2,1)S(1)} %copy-done.5, f32[128,128]{1,0:T(8,128)S(1)} %get-tuple-element.7.weights_ref), custom_call_target="tpu_custom_call" | custom-call | flops 7516192768 | bytes 24117248 | tf_op jit(solution)/shard_map/expert/pallas_call | solution.py:191
  129.8 14.7 %all_to_all.10 = f32[128,1,128]{2,1,0:T(1,128)S(1)} all-to-all(f32[128,1,128]{2,1,0:T(1,128)S(1)} %bitcast.9), channel_id=1, replica_groups=mesh['node'=4,'expert'=32] {'node','expert'}, dimensions={0} | all-to-all | bytes 131072 | tf_op jit(solution)/shard_map/all_to_all | solution.py:214
  144.5 2.2 %final.1 = (bf16[1,512,1024]{2,1,0:T(8,128)(2,1)}, f32[32,128]{1,0:T(8,128)}) custom-call(f32[512,1024]{1,0:T(8,128)S(1)} %get-tuple-element.8.raw_ref, f32[128,128]{1,0:T(8,128)S(1)} %bitcast.8, f32[32,128]{1,0:T(8,128)S(1)} %get-tuple-element.10.rank_ref, f32[32,128]{1,0:T(8,128)S(1)} %get-tuple-element.11.chosen_ref), custom_call_target="tpu_custom_call" | custom-call | tf_op jit(solution)/shard_map/final/pallas_call | solution.py:218
Async XLA Ops:
  0.6 1.0 copy-start.1
  1.6 0.7 copy-start.2
  7.0 3.0 %copy-start = (bf16[2048,1792]{1,0:T(8,128)(2,1)}, bf16[2048,1792]{1,0:T(8,128)(2,1)S(1)}, u32[]{:S(2)}) copy-start(bf16[2048,1792]{1,0:T(8,128)(2,1)S(1)} %pack.1) | copy-start | bytes 22020100
  10.0 11.9 %copy-start.3 = (s32[32,8]{0,1:T(8,128)S(1)}, s32[32,8]{0,1:T(8,128)}, u32[]{:S(2)}) copy-start(s32[32,8]{0,1:T(8,128)} %param.7) | copy-start | bytes 3076
  10.0 11.9 %copy-start.4 = (f32[32,128]{1,0:T(8,128)S(1)}, f32[32,128]{1,0:T(8,128)}, u32[]{:S(2)}) copy-start(f32[32,128]{1,0:T(8,128)} %logits_ref.1) | copy-start | bytes 49156
  10.0 104.5 %copy-start.5 = (bf16[1,512,1024]{2,1,0:T(8,128)(2,1)S(1)}, bf16[1,512,1024]{2,1,0:T(8,128)(2,1)}, u32[]{:S(2)}) copy-start(bf16[1,512,1024]{2,1,0:T(8,128)(2,1)} %hidden_ref.1) | copy-start | bytes 3145732
  10.0 104.5 %all-to-all-start = ((bf16[128,16,1792]{2,1,0:T(8,128)(2,1)}), bf16[128,16,1792]{2,1,0:T(8,128)(2,1)}, u32[]{:S(2)}, u32[]{:S(2)}) async-start(bf16[128,16,1792]{2,1,0:T(8,128)(2,1)} %bitcast.7), calls=%async_computation | async-start | bytes 14680064 | tf_op jit(solution)/shard_map/all_to_all | solution.py:177

commit v2 on v1

--- a/solution.py
+++ b/solution.py
@@ -28,31 +28,41 @@
     return picked * (earlier + 1.0)
 
 
-def pack_kernel(slots, routes_ref, grad_ref, out_ref, ranks, pieces):
+def pack_kernel(slots, routes_ref, grad_ref, out_hbm, ranks, pieces, out, sems):
     tokens, width = grad_ref.shape
     experts = ranks.shape[0]
     span = QUARTERS * PIECE
-
-    @pl.when(pl.program_id(0) == 0)
-    def _():
-        found = slot_ranks(routes_ref[...], experts).astype(jnp.bfloat16)
-        ranks[...] = jnp.concatenate([found] * QUARTERS, 1)
-        for step in range(width // span):
-            for q in range(QUARTERS):
-                pieces[q * tokens : (q + 1) * tokens, step * PIECE : (step + 1) * PIECE] = grad_ref[
-                    :, step * span + q * PIECE : step * span + (q + 1) * PIECE
-                ]
-
-    rows, columns = out_ref.shape[0], QUARTERS * tokens
-    unit = QUARTERS * slots
-    row = iota((rows, experts), 0) + pl.program_id(0) * rows
-    spread = (row // unit == iota((rows, experts), 1)).astype(jnp.bfloat16)
-    rank = jnp.dot(spread, ranks[...], preferred_element_type=jnp.float32)
-    row = iota((rows, columns), 0)
-    slot = (row % slots + 1).astype(jnp.float32)
-    same = (row // slots) % QUARTERS == iota((rows, columns), 1) // tokens
-    take = jnp.where(same & (rank == slot), 1.0, 0.0).astype(jnp.bfloat16)
-    out_ref[...] = jnp.dot(take, pieces[...], preferred_element_type=jnp.float32).astype(jnp.bfloat16)
+    found = slot_ranks(routes_ref[...], experts).astype(jnp.bfloat16)
+    ranks[...] = jnp.concatenate([found] * QUARTERS, 1)
+    for step in range(width // span):
+        for q in range(QUARTERS):
+            pieces[q * tokens : (q + 1) * tokens, step * PIECE : (step + 1) * PIECE] = grad_ref[
+                :, step * span + q * PIECE : step * span + (q + 1) * PIECE
+            ]
+    blocks = sems.shape[0]
+    rows, columns = out.shape[0] // blocks, QUARTERS * tokens
+    unit = QUARTERS * slots
+
+    def copy(b):
+        at = pl.ds(pl.multiple_of(b * rows, rows), rows)
+        return pltpu.make_async_copy(out.at[at, :], out_hbm.at[at, :], sems.at[b])
+
+    @pl.loop(0, blocks)
+    def _(b):
+        row = iota((rows, experts), 0) + b * rows
+        spread = (row // unit == iota((rows, experts), 1)).astype(jnp.bfloat16)
+        rank = jnp.dot(spread, ranks[...], preferred_element_type=jnp.float32)
+        row = iota((rows, columns), 0)
+        slot = (row % slots + 1).astype(jnp.float32)
+        same = (row // slots) % QUARTERS == iota((rows, columns), 1) // tokens
+        take = jnp.where(same & (rank == slot), 1.0, 0.0).astype(jnp.bfloat16)
+        at = pl.ds(pl.multiple_of(b * rows, rows), rows)
+        out[at, :] = jnp.dot(take, pieces[...], preferred_element_type=jnp.float32).astype(jnp.bfloat16)
+        copy(b).start()
+
+    @pl.loop(0, blocks)
+    def _(b):
+        copy(b).wait()
 
 
 def weight_kernel(slots, routes_ref, logits_ref, out_ref, rank_ref, chosen_ref):
@@ -74,42 +84,104 @@
     out_ref[...] = out
 
 
-def expert_kernel(slots, rows_ref, w_ref, hidden_ref, weights_ref, raw_ref, back_ref, rows):
-    unit = QUARTERS * slots
-    step = pl.program_id(0)
+def project_kernel(slots, hidden_ref, w_ref, out_ref):
     block = 256
     each = block // QUARTERS
+    unit = QUARTERS * slots
+    to, came = iota((block, block), 0), iota((block, block), 1)
+    source = (to // slots) % QUARTERS * each + to // unit * slots + to % slots
+    order = (came == source).astype(jnp.bfloat16)
+    whole = jnp.dot(hidden_ref[...], w_ref[...], preferred_element_type=jnp.float32).astype(jnp.bfloat16)
+    for b in range(out_ref.shape[0] // block):
+        rows = whole[b * each : (b + 1) * each]
+        stacked = jnp.concatenate([rows[:, q * PIECE : (q + 1) * PIECE] for q in range(QUARTERS)], 0)
+        out_ref[b * block : (b + 1) * block, :] = jnp.dot(
+            order, stacked, preferred_element_type=jnp.float32
+        ).astype(jnp.bfloat16)
+
+
+def return_kernel(slots, rows_hbm, project_hbm, weights_ref, back_ref, rows, project, row_sems, project_sems):
+    blocks = row_sems.shape[0]
+    block, narrow = rows.shape[0] // blocks, rows.shape[1]
+    unit = QUARTERS * slots
+    lanes = back_ref.shape[1]
+    part = 128
+
+    def copies(b):
+        at = pl.ds(pl.multiple_of(b * block, block), block)
+        return (
+            pltpu.make_async_copy(rows_hbm.at[at, :], rows.at[at, :], row_sems.at[b]),
+            pltpu.make_async_copy(project_hbm.at[at, :], project.at[at, :], project_sems.at[b]),
+        )
+
+    for b in range(blocks):
+        for copy in copies(b):
+            copy.start()
+
+    @pl.loop(0, blocks)
+    def _(b):
+        for copy in copies(b):
+            copy.wait()
+        for start in range(0, block, part):
+            at = pl.ds(pl.multiple_of(b * block + start, part), part)
+            product = rows[at, :].astype(jnp.float32) * project[at, :].astype(jnp.float32)
+            total = product[:, :lanes]
+            for column in range(lanes, narrow, lanes):
+                total += product[:, column : column + lanes]
+            grads = jnp.sum(total, 1, keepdims=True)
+            slot = iota((part, lanes), 0) % slots
+            spread = jnp.where(slot == iota((part, lanes), 1), grads, 0.0)
+            peers = part // unit
+            to = pl.ds(pl.multiple_of(b * (block // unit) + start // unit, peers), peers)
+            back_ref[to, :] = weights_ref[to, :] + jnp.sum(spread.reshape(peers, unit, lanes), 1)
+
+
+def expert_kernel(slots, rows_hbm, w_hbm, raw_ref, arrived, rows, w, row_sems, w_sems):
+    block = 256
+    each = block // QUARTERS
+    unit = QUARTERS * slots
+    blocks = arrived.shape[0] // block
+    tiles = w_sems.shape[0]
+    tile = w.shape[0] // tiles
+
+    def row_copy(b):
+        at = pl.ds(pl.multiple_of(b * block, block), block)
+        return pltpu.make_async_copy(rows_hbm.at[at, :], arrived.at[at, :], row_sems.at[b])
+
+    def w_copy(n):
+        at = pl.ds(pl.multiple_of(n * tile, tile), tile)
+        return pltpu.make_async_copy(w_hbm.at[0, at, :], w.at[at, :], w_sems.at[n])
+
+    for b in range(blocks):
+        row_copy(b).start()
     to, came = iota((block, block), 0), iota((block, block), 1)
     source = (to % each) // slots * unit + to // each * slots + to % slots
     order = (came == source).astype(jnp.bfloat16)
-    for b in range(rows_ref.shape[0] // block):
-        turned = jnp.dot(
-            order, rows_ref[b * block : (b + 1) * block, :], preferred_element_type=jnp.float32
-        ).astype(jnp.bfloat16)
-        for q in range(QUARTERS):
-            rows[b * each : (b + 1) * each, q * PIECE : (q + 1) * PIECE] = turned[q * each : (q + 1) * each]
-    part = lax.dot_general(
-        rows[...], w_ref[...], (((1,), (1,)), ((), ())), preferred_element_type=jnp.float32
-    )
-
-    @pl.when(step == 0)
-    def _():
-        raw_ref[...] = part
-
-    @pl.when(step > 0)
-    def _():
-        raw_ref[...] += part
-
-    @pl.when(step == pl.num_programs(0) - 1)
-    def _():
-        capacity = raw_ref.shape[0]
-        peers, lanes = back_ref.shape
-        grads = jnp.sum(raw_ref[...] * hidden_ref[...].astype(jnp.float32), 1, keepdims=True)
-        slot = iota((capacity, lanes), 0) % slots
-        spread = jnp.where(slot == iota((capacity, lanes), 1), grads, 0.0)
-        gather = (iota((peers, capacity), 0) == iota((peers, capacity), 1) // slots).astype(jnp.float32)
-        back_ref[...] = weights_ref[...] + jnp.dot(
-            gather, spread, preferred_element_type=jnp.float32, precision=lax.Precision.HIGHEST
+
+    @pl.loop(0, blocks)
+    def _(b):
+        row_copy(b).wait()
+
+        @pl.when(b % (blocks // tiles) == blocks // tiles - 1)
+        def _():
+            w_copy(b // (blocks // tiles)).start()
+
+        at = pl.ds(pl.multiple_of(b * block, block), block)
+        to = pl.ds(pl.multiple_of(b * each, each), each)
+        for step in range(arrived.shape[1] // PIECE):
+            turned = jnp.dot(
+                order, arrived[at, step * PIECE : (step + 1) * PIECE], preferred_element_type=jnp.float32
+            ).astype(jnp.bfloat16)
+            for q in range(QUARTERS):
+                column = (step * QUARTERS + q) * PIECE
+                rows[to, column : column + PIECE] = turned[q * each : (q + 1) * each]
+
+    @pl.loop(0, tiles)
+    def _(n):
+        w_copy(n).wait()
+        at = pl.ds(pl.multiple_of(n * tile, tile), tile)
+        raw_ref[:, at] = lax.dot_general(
+            rows[...], w[at, :], (((1,), (1,)), ((), ())), preferred_element_type=jnp.float32
         )
 
 
@@ -143,8 +215,12 @@
     return pl.BlockSpec(shape, lambda i: (0,) * len(shape))
 
 
-def params():
-    return pltpu.CompilerParams(vmem_limit_bytes=40 * MIB)
+def params(size=24):
+    return pltpu.CompilerParams(vmem_limit_bytes=size * MIB)
+
+
+def in_hbm(array):
+    return pltpu.with_memory_space_constraint(array, pltpu.HBM)
 
 
 def shards(grad_out, logits, routes, w_down, saved_hidden):
@@ -155,16 +231,17 @@
     unit = QUARTERS * slots
     narrow = width // QUARTERS
     routes_t = routes.T
-    pack_rows = 256
+    near, far = pl.BlockSpec(memory_space=pltpu.VMEM), pl.BlockSpec(memory_space=pltpu.HBM)
     sent = pl.pallas_call(
         functools.partial(pack_kernel, slots),
-        grid=(experts * unit // pack_rows,),
-        in_specs=[whole(routes_t.shape), whole(grad_out.shape)],
-        out_specs=pl.BlockSpec((pack_rows, narrow), lambda i: (i, 0)),
-        out_shape=jax.ShapeDtypeStruct((experts * unit, narrow), jnp.bfloat16),
+        in_specs=[near, near],
+        out_specs=far,
+        out_shape=pltpu.HBM((experts * unit, narrow), jnp.bfloat16),
         scratch_shapes=[
             pltpu.VMEM((experts, QUARTERS * tokens), jnp.bfloat16),
             pltpu.VMEM((QUARTERS * tokens, narrow), jnp.bfloat16),
+            pltpu.VMEM((experts * unit, narrow), jnp.bfloat16),
+            pltpu.SemaphoreType.DMA((8,)),
         ],
         compiler_params=params(),
         cost_estimate=pl.CostEstimate(
@@ -173,7 +250,7 @@
             transcendentals=0,
         ),
         name="pack",
-    )(routes_t, grad_out)
+    )(in_hbm(routes_t), in_hbm(grad_out))
     arrived = lax.all_to_all(
         sent.reshape(experts, unit, narrow), ("node", "expert"), split_axis=0, concat_axis=0, tiled=True
     ).reshape(experts * unit, narrow)
@@ -188,29 +265,57 @@
         name="weights",
     )(routes_t, logits)
     span = QUARTERS * PIECE
-    raw, back = pl.pallas_call(
-        functools.partial(expert_kernel, slots),
+    project = pl.pallas_call(
+        functools.partial(project_kernel, slots),
         grid=(width // span,),
         in_specs=[
-            pl.BlockSpec((experts * unit, PIECE), lambda i: (0, i)),
+            pl.BlockSpec((None, capacity, units), lambda i: (0, 0, 0)),
             pl.BlockSpec((None, units, span), lambda i: (0, 0, i)),
-            pl.BlockSpec((None, capacity, units), lambda i: (0, 0, 0)),
-            whole((experts, experts)),
-        ],
-        out_specs=(whole((capacity, units)), whole((experts, experts))),
-        out_shape=(
-            jax.ShapeDtypeStruct((capacity, units), jnp.float32),
-            jax.ShapeDtypeStruct((experts, experts), jnp.float32),
-        ),
-        scratch_shapes=[pltpu.VMEM((capacity, span), jnp.bfloat16)],
-        compiler_params=params(),
+        ],
+        out_specs=pl.BlockSpec((experts * unit, PIECE), lambda i: (0, i)),
+        out_shape=pltpu.HBM((experts * unit, narrow), jnp.bfloat16),
+        compiler_params=params(),
+        cost_estimate=pl.CostEstimate(
+            flops=2 * capacity * units * width, bytes_accessed=2 * units * width, transcendentals=0
+        ),
+        name="project",
+    )(saved_hidden, in_hbm(w_down))
+    back = pl.pallas_call(
+        functools.partial(return_kernel, slots),
+        in_specs=[far, far, near],
+        out_specs=near,
+        out_shape=jax.ShapeDtypeStruct((experts, experts), jnp.float32),
+        scratch_shapes=[
+            pltpu.VMEM((experts * unit, narrow), jnp.bfloat16),
+            pltpu.VMEM((experts * unit, narrow), jnp.bfloat16),
+            pltpu.SemaphoreType.DMA((8,)),
+            pltpu.SemaphoreType.DMA((8,)),
+        ],
+        compiler_params=params(),
+        cost_estimate=pl.CostEstimate(
+            flops=2 * capacity * width, bytes_accessed=4 * capacity * width, transcendentals=0
+        ),
+        name="return",
+    )(in_hbm(arrived), in_hbm(project), weights)
+    raw = pl.pallas_call(
+        functools.partial(expert_kernel, slots),
+        in_specs=[far, far],
+        out_shape=jax.ShapeDtypeStruct((capacity, units), jnp.float32),
+        scratch_shapes=[
+            pltpu.VMEM((experts * unit, narrow), jnp.bfloat16),
+            pltpu.VMEM((capacity, width), jnp.bfloat16),
+            pltpu.VMEM((units, width), jnp.bfloat16),
+            pltpu.SemaphoreType.DMA((experts * unit // 256,)),
+            pltpu.SemaphoreType.DMA((units // 256,)),
+        ],
+        compiler_params=params(48),
         cost_estimate=pl.CostEstimate(
             flops=2 * capacity * units * width,
             bytes_accessed=2 * (units + capacity) * width + 4 * capacity * units,
             transcendentals=0,
         ),
         name="expert",
-    )(arrived, w_down, saved_hidden, weights)
+    )(in_hbm(arrived), in_hbm(w_down))
     returned = lax.all_to_all(
         back.reshape(experts, 1, experts), ("node", "expert"), split_axis=0, concat_axis=0, tiled=True
     ).reshape(experts, experts)

time: 147 us -> 139 us (0.946)
  Pallas kernels: 22.8 us -> 43.6 us
  waiting for transfers between devices: 92 us -> 77.1 us
  blocking collectives: 14.7 us -> 0 us
  starting transfers between devices: 11.9 us -> 17.3 us
  local copies, waits for them, and re-layouts: 4.71 us -> 0.02 us
    pallas_call x2 -> x4, Pallas kernels: 19.9 us -> 40.7 us  [the longest x1 14.8 us: shards(): pl.pallas_call(functools.partial(project_kernel, slots), grid=(width // s...]
    all_to_all x1, waiting for transfers between devices: 92 us -> 77.1 us  [shards(): lax.all_to_all(sent.reshape(experts, unit, narrow), ('node', 'expert'), s...]
    all_to_all x1 -> x0, blocking collectives: 14.7 us -> none  [shards(): lax.all_to_all(back.reshape(experts, 1, experts), ('node', 'expert'), spl...]
    all_to_all x0 -> x1, starting transfers between devices: none -> 5.37 us  [shards(): lax.all_to_all(back.reshape(experts, 1, experts), ('node', 'expert'), spl...]
    unnamed x12 -> x6, local copies, waits for them, and re-layouts: 4.71 us -> 0.02 us
  transfers between devices with their start and end apart: 1 -> 2, of which waited for: 1 -> 1; matrix products, arithmetic and copies ran while one was open for 0% -> 0% of each run, Pallas kernels for 0% -> 20%
where the time goes in v2:
time: 139 us
  waiting for transfers between devices  77.1 us (55%)
  Pallas kernels  43.6 us (31%)
  starting transfers between devices  17.3 us (12%)
    all_to_all x1, waiting for transfers between devices, shards(): lax.all_to_all(sent.reshape(experts, unit, narrow), ('node', 'expert'), s...  77.1 us
    pallas_call x1, Pallas kernels, shards(): pl.pallas_call(functools.partial(project_kernel, slots), grid=(width // s...  14.8 us
    pallas_call x1, Pallas kernels, shards(): pl.pallas_call(functools.partial(expert_kernel, slots), in_specs=[far, fa...  13 us
    all_to_all x1, starting transfers between devices, shards(): lax.all_to_all(sent.reshape(experts, unit, narrow), ('node', 'expert'), s...  11.9 us
    pallas_call x1, Pallas kernels, shards(): pl.pallas_call(functools.partial(pack_kernel, slots), in_specs=[near, nea...  6.66 us
    pallas_call x1, Pallas kernels, shards(): pl.pallas_call(functools.partial(return_kernel, slots), in_specs=[far, fa...  6.28 us
    all_to_all x1, starting transfers between devices, shards(): lax.all_to_all(back.reshape(experts, 1, experts), ('node', 'expert'), spl...  5.37 us
  transfers between devices with their start and end apart: 2, of which 1 were waited for; matrix products, arithmetic and copies ran while one was open for 0% of the time, Pallas kernels for 20%

profile of v2, /device:TPU:1, one launch (start us, length us, event | category | flops | bytes accessed | tf_op | source)
XLA Modules:
  0.0 138.8 jit_solution(14485448093792670391)
XLA Ops:
  0.6 6.7 %pack.1 = bf16[2048,1792]{1,0:T(8,128)(2,1)} custom-call(s32[8,32]{1,0:T(8,128)} %bitcast.8, bf16[32,7168]{1,0:T(8,128)(2,1)} %grad_ref.1), custom_call_target="tpu_custom_call" | custom-call | flops 939524096 | bytes 7340032 | tf_op jit(solution)/shard_map/pack/pallas_call | solution.py:235
  7.3 0.0 copy-start
  7.3 0.0 copy-start.1
  7.3 0.0 copy-start.2
  7.3 11.9 %all-to-all-start = ((bf16[128,16,1792]{2,1,0:T(8,128)(2,1)}), bf16[128,16,1792]{2,1,0:T(8,128)(2,1)}, u32[]{:S(2)}, u32[]{:S(2)}) async-start(bf16[128,16,1792]{2,1,0:T(8,128)(2,1)} %bitcast.10), calls=%async_computation | async-start | bytes 14680064 | tf_op jit(solution)/shard_map/all_to_all | solution.py:254
  19.2 0.0 copy-done
  19.3 0.0 copy-done.1
  19.3 0.6 weights.1
  19.9 0.0 copy-done.2
  19.9 14.8 %project.1.project_hbm = bf16[2048,1792]{1,0:T(8,128)(2,1)} custom-call(bf16[1,512,1024]{2,1,0:T(8,128)(2,1)S(1)} %copy-done.2, bf16[1,1024,7168]{2,1,0:T(8,128)(2,1)} %w_ref.1), custom_call_target="tpu_custom_call" | custom-call | flops 7516192768 | bytes 14680064 | tf_op jit(solution)/shard_map/project/pallas_call | solution.py:268
  34.7 77.1 %all-to-all-done = bf16[128,16,1792]{2,1,0:T(8,128)(2,1)} async-done(((bf16[128,16,1792]{2,1,0:T(8,128)(2,1)}), bf16[128,16,1792]{2,1,0:T(8,128)(2,1)}, u32[]{:S(2)}, u32[]{:S(2)}) %all-to-all-start) | async-done | bytes 7340064 | tf_op jit(solution)/shard_map/all_to_all | solution.py:254
  111.9 6.3 %return.1 = f32[128,128]{1,0:T(8,128)} custom-call(bf16[2048,1792]{1,0:T(8,128)(2,1)} %bitcast.2.rows_hbm, bf16[2048,1792]{1,0:T(8,128)(2,1)} %project.1.project_hbm, f32[128,128]{1,0:T(8,128)S(1)} %get-tuple-element.5.weights_ref), custom_call_target="tpu_custom_call" | custom-call | flops 7340032 | bytes 14680064 | tf_op jit(solution)/shard_map/return/pallas_call | solution.py:283
  118.2 5.4 %all-to-all-start.1 = ((f32[128,1,128]{2,1,0:T(1,128)}), f32[128,1,128]{2,1,0:T(1,128)S(1)}, u32[]{:S(2)}, u32[]{:S(2)}) async-start(f32[128,1,128]{2,1,0:T(1,128)} %bitcast.4), calls=%async_computation.1 | async-start | bytes 131072 | tf_op jit(solution)/shard_map/all_to_all | solution.py:319
  123.5 13.0 %expert.1.raw_ref = f32[512,1024]{1,0:T(8,128)S(1)} custom-call(bf16[2048,1792]{1,0:T(8,128)(2,1)} %bitcast.2.rows_hbm, bf16[1,1024,7168]{2,1,0:T(8,128)(2,1)} %w_ref.1), custom_call_target="tpu_custom_call" | custom-call | flops 7516192768 | bytes 24117248 | tf_op jit(solution)/shard_map/expert/pallas_call | solution.py:300
  136.5 0.0 all-to-all-done.1
  136.5 2.3 %final.1 = (bf16[1,512,1024]{2,1,0:T(8,128)(2,1)}, f32[32,128]{1,0:T(8,128)}) custom-call(f32[512,1024]{1,0:T(8,128)S(1)} %expert.1.raw_ref, f32[128,128]{1,0:T(8,128)S(1)} %bitcast.7, f32[32,128]{1,0:T(8,128)S(1)} %get-tuple-element.6.rank_ref, f32[32,128]{1,0:T(8,128)S(1)} %get-tuple-element.7.chosen_ref), custom_call_target="tpu_custom_call" | custom-call | tf_op jit(solution)/shard_map/final/pallas_call | solution.py:323
Async XLA Ops:
  7.3 11.9 %copy-start = (s32[32,8]{0,1:T(8,128)S(1)}, s32[32,8]{0,1:T(8,128)}, u32[]{:S(2)}) copy-start(s32[32,8]{0,1:T(8,128)} %param.7) | copy-start | bytes 3076
  7.3 11.9 %copy-start.1 = (f32[32,128]{1,0:T(8,128)S(1)}, f32[32,128]{1,0:T(8,128)}, u32[]{:S(2)}) copy-start(f32[32,128]{1,0:T(8,128)} %logits_ref.1) | copy-start | bytes 49156
  7.3 12.6 %copy-start.2 = (bf16[1,512,1024]{2,1,0:T(8,128)(2,1)S(1)}, bf16[1,512,1024]{2,1,0:T(8,128)(2,1)}, u32[]{:S(2)}) copy-start(bf16[1,512,1024]{2,1,0:T(8,128)(2,1)} %hidden_ref.1) | copy-start | bytes 3145732
  7.3 104.5 %all-to-all-start = ((bf16[128,16,1792]{2,1,0:T(8,128)(2,1)}), bf16[128,16,1792]{2,1,0:T(8,128)(2,1)}, u32[]{:S(2)}, u32[]{:S(2)}) async-start(bf16[128,16,1792]{2,1,0:T(8,128)(2,1)} %bitcast.10), calls=%async_computation | async-start | bytes 14680064 | tf_op jit(solution)/shard_map/all_to_all | solution.py:254
  118.2 18.3 %all-to-all-start.1 = ((f32[128,1,128]{2,1,0:T(1,128)}), f32[128,1,128]{2,1,0:T(1,128)S(1)}, u32[]{:S(2)}, u32[]{:S(2)}) async-start(f32[128,1,128]{2,1,0:T(1,128)} %bitcast.4), calls=%async_computation.1 | async-start | bytes 131072 | tf_op jit(solution)/shard_map/all_to_all | solution.py:319

commit v3 on v2

v3 whole, which is shorter than its diff:
```python
import functools

import jax
import jax.numpy as jnp
from jax import lax
from jax.experimental import pallas as pl
from jax.experimental.pallas import tpu as pltpu
from jax.sharding import PartitionSpec as P

route_scale = 2.5
MIB = 1 << 20


def iota(shape, dim):
    return lax.broadcasted_iota(jnp.int32, shape, dim)


def slot_ranks(routes_t, experts):
    most, tokens = routes_t.shape
    ids = iota((experts, tokens), 0)
    picked = jnp.zeros((experts, tokens), jnp.float32)
    for k in range(most):
        picked += (routes_t[k : k + 1, :] == ids).astype(jnp.float32)
    before = (iota((tokens, tokens), 0) < iota((tokens, tokens), 1)).astype(jnp.bfloat16)
    earlier = jnp.dot(picked.astype(jnp.bfloat16), before, preferred_element_type=jnp.float32)
    return picked * (earlier + 1.0)


def pack_kernel(slots, routes_ref, grad_ref, out_hbm, out, sems):
    tokens, width = grad_ref.shape
    experts = out.shape[0]
    rows = experts * slots
    rank = slot_ranks(routes_ref[...], experts)
    rank = jnp.broadcast_to(rank[:, None, :], (experts, slots, tokens)).reshape(rows, tokens)
    slot = (iota((rows, tokens), 0) % slots + 1).astype(jnp.float32)
    take = jnp.where(rank == slot, 1.0, 0.0).astype(jnp.bfloat16)
    parts = sems.shape[0]
    part = width // parts

    def copy(c):
        at = pl.ds(c * part, part)
        return pltpu.make_async_copy(out.at[:, :, at], out_hbm.at[:, :, at], sems.at[c])

    for c in range(parts):
        at = pl.ds(c * part, part)
        packed = jnp.dot(take, grad_ref[:, at], preferred_element_type=jnp.float32).astype(jnp.bfloat16)
        out[:, :, at] = packed.reshape(experts, slots, part)
        copy(c).start()
    for c in range(parts):
        copy(c).wait()


def weight_kernel(slots, routes_ref, logits_ref, out_ref, rank_ref, chosen_ref):
    tokens, experts = logits_ref.shape
    found = slot_ranks(routes_ref[...], experts).astype(jnp.bfloat16)
    unit = (iota((experts, experts), 0) == iota((experts, experts), 1)).astype(jnp.bfloat16)
    rank = lax.dot_general(found, unit, (((0,), (0,)), ((), ())), preferred_element_type=jnp.float32)
    rank_ref[...] = rank
    chosen = jnp.where(rank > 0.0, jax.nn.sigmoid(logits_ref[...]), 0.0)
    chosen_ref[...] = chosen
    total = jnp.sum(chosen, 1, keepdims=True)
    weights = (route_scale * chosen / total).astype(jnp.bfloat16).astype(jnp.float32)
    out = jnp.zeros((experts, experts), jnp.float32)
    lane = iota((tokens, experts), 1)
    for j in range(slots):
        mine = jnp.where(rank == j + 1.0, weights, 0.0).astype(jnp.bfloat16)
        to = (lane == slots + j).astype(jnp.bfloat16)
        out += lax.dot_general(mine, to, (((0,), (0,)), ((), ())), preferred_element_type=jnp.float32)
    out_ref[...] = out


def project_kernel(hidden_ref, w_ref, out_ref):
    out_ref[...] = jnp.dot(hidden_ref[...], w_ref[...], preferred_element_type=jnp.float32).astype(jnp.bfloat16)


def return_kernel(rows_hbm, project_hbm, weights_ref, back_ref, rows, project, row_sems, project_sems):
    blocks = row_sems.shape[0]
    slots, width = rows.shape[1:]
    peers = rows.shape[0] // blocks
    lanes = back_ref.shape[1]
    part, wide = 8, 1024

    def copies(b):
        at = pl.ds(pl.multiple_of(b * peers, peers), peers)
        to = pl.ds(pl.multiple_of(b * peers * slots, peers * slots), peers * slots)
        return (
            pltpu.make_async_copy(rows_hbm.at[at], rows.at[at], row_sems.at[b]),
            pltpu.make_async_copy(project_hbm.at[to, :], project.at[to, :], project_sems.at[b]),
        )

    for b in range(blocks):
        for copy in copies(b):
            copy.start()

    @pl.loop(0, blocks)
    def _(b):
        for copy in copies(b):
            copy.wait()
        for start in range(0, peers, part):
            at = pl.ds(pl.multiple_of(b * peers + start, part), part)
            to = pl.ds(pl.multiple_of((b * peers + start) * slots, part * slots), part * slots)
            total = jnp.zeros((part * slots, lanes), jnp.float32)
            for begin in range(0, width, wide):
                columns = slice(begin, begin + wide)
                row = rows[at, :, columns].reshape(part * slots, wide).astype(jnp.float32)
                product = row * project[to, columns].astype(jnp.float32)
                for column in range(0, wide, lanes):
                    total += product[:, column : column + lanes]
            grads = jnp.sum(total, 1, keepdims=True)
            slot = iota((part * slots, lanes), 0) % slots
            spread = jnp.where(slot == iota((part * slots, lanes), 1), grads, 0.0)
            back_ref[at, :] = weights_ref[at, :] + jnp.sum(spread.reshape(part, slots, lanes), 1)


def expert_kernel(rows_hbm, w_hbm, raw_ref, arrived, rows, w, row_sems, w_sems):
    blocks, tiles = row_sems.shape[0], w_sems.shape[0]
    peers = arrived.shape[0] // blocks
    slots, width = arrived.shape[1:]
    tile = w.shape[0] // tiles

    def row_copy(b):
        at = pl.ds(pl.multiple_of(b * peers, peers), peers)
        return pltpu.make_async_copy(rows_hbm.at[at], arrived.at[at], row_sems.at[b])

    def w_copy(n):
        at = pl.ds(pl.multiple_of(n * tile, tile), tile)
        return pltpu.make_async_copy(w_hbm.at[0, at, :], w.at[at, :], w_sems.at[n])

    halves = 2
    group = blocks // halves
    half = group * peers * slots

    def product(at, n):
        to = pl.ds(pl.multiple_of(n * tile, tile), tile)
        raw_ref[at, to] = lax.dot_general(
            rows[at, :], w[to, :], (((1,), (1,)), ((), ())), preferred_element_type=jnp.float32
        )

    for b in range(group):
        row_copy(b).start()
    w_copy(0).start()

    @pl.loop(0, halves)
    def _(h):
        @pl.loop(0, group)
        def _(g):
            b = h * group + g
            row_copy(b).wait()

            @pl.when(h == 0)
            def _():
                row_copy(group + g).start()

            at = pl.ds(pl.multiple_of(b * peers, peers), peers)
            to = pl.ds(pl.multiple_of(b * peers * slots, peers * slots), peers * slots)
            rows[to, :] = arrived[at].reshape(peers * slots, width)

        @pl.when(h == 0)
        def _():
            w_copy(0).wait()
            w_copy(1).start()

        product(pl.ds(pl.multiple_of(h * half, half), half), 0)

    @pl.loop(1, tiles)
    def _(n):
        w_copy(n).wait()

        @pl.when(n < tiles - 1)
        def _():
            w_copy(n + 1).start()

        product(slice(None), n)


def final_kernel(
    slots, raw_ref, back_ref, rank_ref, chosen_ref, hidden_hbm, logits_ref, hidden, out_sems
):
    blocks = out_sems.shape[0]
    block = raw_ref.shape[0] // blocks
    peers = block // slots
    lanes = back_ref.shape[1]

    def out_copy(b):
        at = pl.ds(b * block, block)
        return pltpu.make_async_copy(hidden.at[at, :], hidden_hbm.at[0, at, :], out_sems.at[b])

    spread = (iota((block, peers), 0) // slots == iota((block, peers), 1)).astype(jnp.bfloat16)
    slot = iota((block, lanes), 0) % slots
    mine = slot + slots == iota((block, lanes), 1)
    for b in range(blocks):
        sent = back_ref[b * peers : (b + 1) * peers, :].astype(jnp.bfloat16)
        weight = jnp.dot(spread, sent, preferred_element_type=jnp.float32)
        weight = jnp.sum(jnp.where(mine, weight, 0.0), 1, keepdims=True)
        at = slice(b * block, (b + 1) * block)
        hidden[at, :] = (weight * raw_ref[at, :]).astype(jnp.bfloat16)
        out_copy(b).start()
    rank = rank_ref[...]
    chosen = chosen_ref[...]
    total = jnp.sum(chosen, 1, keepdims=True)
    back = jnp.transpose(back_ref[...])
    per_route = jnp.zeros_like(chosen)
    for j in range(slots):
        per_route += jnp.where(rank == j + 1.0, back[j : j + 1, :], 0.0)
    mean_grad = jnp.sum(per_route * chosen, 1, keepdims=True) / total
    d_chosen = (route_scale / total) * (per_route - mean_grad)
    logits_ref[...] = jnp.where(rank > 0.0, d_chosen * chosen * (1.0 - chosen), 0.0)
    for b in range(blocks):
        out_copy(b).wait()


def params(size=24):
    return pltpu.CompilerParams(vmem_limit_bytes=size * MIB)


def in_hbm(array):
    return pltpu.with_memory_space_constraint(array, pltpu.HBM)


def shards(grad_out, logits, routes, w_down, saved_hidden):
    tokens, width = grad_out.shape
    experts = logits.shape[1]
    capacity, units = saved_hidden.shape[1:]
    slots = capacity // experts
    routes_t = routes.T
    near, far = pl.BlockSpec(memory_space=pltpu.VMEM), pl.BlockSpec(memory_space=pltpu.HBM)
    packed = (experts, slots, width)
    sent = pl.pallas_call(
        functools.partial(pack_kernel, slots),
        in_specs=[near, near],
        out_specs=far,
        out_shape=pltpu.HBM(packed, jnp.bfloat16),
        scratch_shapes=[pltpu.VMEM(packed, jnp.bfloat16), pltpu.SemaphoreType.DMA((7,))],
        compiler_params=params(),
        cost_estimate=pl.CostEstimate(
            flops=2 * capacity * width * tokens, bytes_accessed=2 * capacity * width, transcendentals=0
        ),
        name="pack",
    )(in_hbm(routes_t), in_hbm(grad_out))
    arrived = lax.all_to_all(sent, ("node", "expert"), split_axis=0, concat_axis=0, tiled=True)
    weights, rank, chosen = pl.pallas_call(
        functools.partial(weight_kernel, slots),
        out_shape=(
            jax.ShapeDtypeStruct((experts, experts), jnp.float32),
            jax.ShapeDtypeStruct((tokens, experts), jnp.float32),
            jax.ShapeDtypeStruct((tokens, experts), jnp.float32),
        ),
        compiler_params=params(),
        name="weights",
    )(routes_t, logits)
    span = 1024
    project = pl.pallas_call(
        project_kernel,
        grid=(width // span,),
        in_specs=[
            pl.BlockSpec((None, capacity, units), lambda i: (0, 0, 0)),
            pl.BlockSpec((None, units, span), lambda i: (0, 0, i)),
        ],
        out_specs=pl.BlockSpec((capacity, span), lambda i: (0, i)),
        out_shape=pltpu.HBM((capacity, width), jnp.bfloat16),
        compiler_params=params(),
        cost_estimate=pl.CostEstimate(
            flops=2 * capacity * units * width, bytes_accessed=2 * units * width, transcendentals=0
        ),
        name="project",
    )(saved_hidden, in_hbm(w_down))
    back = pl.pallas_call(
        return_kernel,
        in_specs=[far, far, near],
        out_specs=near,
        out_shape=jax.ShapeDtypeStruct((experts, experts), jnp.float32),
        scratch_shapes=[
            pltpu.VMEM(packed, jnp.bfloat16),
            pltpu.VMEM((capacity, width), jnp.bfloat16),
            pltpu.SemaphoreType.DMA((8,)),
            pltpu.SemaphoreType.DMA((8,)),
        ],
        compiler_params=params(),
        cost_estimate=pl.CostEstimate(
            flops=2 * capacity * width, bytes_accessed=4 * capacity * width, transcendentals=0
        ),
        name="return",
    )(in_hbm(arrived), in_hbm(project), weights)
    raw = pl.pallas_call(
        expert_kernel,
        in_specs=[far, far],
        out_shape=jax.ShapeDtypeStruct((capacity, units), jnp.float32),
        scratch_shapes=[
            pltpu.VMEM(packed, jnp.bfloat16),
            pltpu.VMEM((capacity, width), jnp.bfloat16),
            pltpu.VMEM((units, width), jnp.bfloat16),
            pltpu.SemaphoreType.DMA((8,)),
            pltpu.SemaphoreType.DMA((units // 256,)),
        ],
        compiler_params=params(48),
        cost_estimate=pl.CostEstimate(
            flops=2 * capacity * units * width,
            bytes_accessed=2 * (units + capacity) * width + 4 * capacity * units,
            transcendentals=0,
        ),
        name="expert",
    )(in_hbm(arrived), in_hbm(w_down))
    returned = lax.all_to_all(
        back.reshape(experts, 1, experts), ("node", "expert"), split_axis=0, concat_axis=0, tiled=True
    ).reshape(experts, experts)
    d_hidden, d_logits = pl.pallas_call(
        functools.partial(final_kernel, slots),
        in_specs=[near, near, near, near],
        out_specs=(far, near),
        out_shape=(
            jax.ShapeDtypeStruct((1, capacity, units), jnp.bfloat16),
            jax.ShapeDtypeStruct((tokens, experts), jnp.float32),
        ),
        scratch_shapes=[
            pltpu.VMEM((capacity, units), jnp.bfloat16),
            pltpu.SemaphoreType.DMA((4,)),
        ],
        compiler_params=params(),
        name="final",
    )(raw, returned, rank, chosen)
    return (d_hidden, d_logits)


def solution(mesh):
    return jax.shard_map(
        shards,
        mesh=mesh,
        in_specs=(
            P(("node", "expert"), None),
            P(("node", "expert"), None),
            P(("node", "expert"), None),
            P(("node", "expert"), None, None),
            P(("node", "expert"), None, None),
        ),
        out_specs=(P(("node", "expert"), None, None), P(("node", "expert"), None)),
        check_vma=False,
    )
```

time: 139 us -> 136 us (0.978)
  Pallas kernels: 43.6 us -> 39.5 us
    pallas_call x4, Pallas kernels: 36.3 us -> 34.3 us  [the longest x1 13.7 us: shards(): pl.pallas_call(project_kernel, grid=(width // span,), in_specs=[pl.BlockS...]
    pallas_call x1, Pallas kernels: 6.66 us -> 4.64 us  [shards(): pl.pallas_call(functools.partial(pack_kernel, slots), in_specs=[near, nea...]
where the time goes in v3:
time: 136 us
  waiting for transfers between devices  78.3 us (58%)
  Pallas kernels  39.5 us (29%)
  starting transfers between devices  17.3 us (13%)
    all_to_all x1, waiting for transfers between devices, shards(): lax.all_to_all(sent, ('node', 'expert'), split_axis=0, concat_axis=0, til...  78.3 us
    pallas_call x1, Pallas kernels, shards(): pl.pallas_call(project_kernel, grid=(width // span,), in_specs=[pl.BlockS...  13.7 us
    pallas_call x1, Pallas kernels, shards(): pl.pallas_call(expert_kernel, in_specs=[far, far], out_shape=jax.ShapeDty...  12.3 us
    all_to_all x1, starting transfers between devices, shards(): lax.all_to_all(sent, ('node', 'expert'), split_axis=0, concat_axis=0, til...  11.9 us
    pallas_call x1, Pallas kernels, shards(): pl.pallas_call(return_kernel, in_specs=[far, far, near], out_specs=near,...  6.46 us
    all_to_all x1, starting transfers between devices, shards(): lax.all_to_all(back.reshape(experts, 1, experts), ('node', 'expert'), spl...  5.37 us
    pallas_call x1, Pallas kernels, shards(): pl.pallas_call(functools.partial(pack_kernel, slots), in_specs=[near, nea...  4.64 us
  transfers between devices with their start and end apart: 2, of which 1 were waited for; matrix products, arithmetic and copies ran while one was open for 0% of the time, Pallas kernels for 20%

profile of v3, /device:TPU:1, one launch (start us, length us, event | category | flops | bytes accessed | tf_op | source)
XLA Modules:
  0.0 135.9 jit_solution(7174962224904538025)
XLA Ops:
  0.6 4.6 %pack.1 = bf16[128,4,7168]{2,1,0:T(4,128)(2,1)} custom-call(s32[8,32]{1,0:T(8,128)} %bitcast.6, bf16[32,7168]{1,0:T(8,128)(2,1)} %grad_ref.1), custom_call_target="tpu_custom_call" | custom-call | flops 234881024 | bytes 7340032 | tf_op jit(solution)/shard_map/pack/pallas_call | solution.py:228
  5.3 0.0 copy-start
  5.3 0.0 copy-start.1
  5.3 0.0 copy-start.2
  5.3 11.9 %all-to-all-start = ((bf16[128,4,7168]{2,1,0:T(4,128)(2,1)}), bf16[128,4,7168]{2,1,0:T(4,128)(2,1)}, u32[]{:S(2)}, u32[]{:S(2)}) async-start(bf16[128,4,7168]{2,1,0:T(4,128)(2,1)} %pack.1), calls=%async_computation | async-start | bytes 14680064 | tf_op jit(solution)/shard_map/all_to_all | solution.py:240
  17.2 0.0 copy-done
  17.2 0.0 copy-done.1
  17.2 0.6 weights.1
  17.9 0.0 copy-done.2
  17.9 13.7 %project.1.project_hbm = bf16[512,7168]{1,0:T(8,128)(2,1)} custom-call(bf16[1,512,1024]{2,1,0:T(8,128)(2,1)S(1)} %copy-done.2, bf16[1,1024,7168]{2,1,0:T(8,128)(2,1)} %w_ref.1), custom_call_target="tpu_custom_call" | custom-call | flops 7516192768 | bytes 14680064 | tf_op jit(solution)/shard_map/project/pallas_call | solution.py:252
  31.6 78.3 %all-to-all-done.rows_hbm = bf16[128,4,7168]{2,1,0:T(4,128)(2,1)} async-done(((bf16[128,4,7168]{2,1,0:T(4,128)(2,1)}), bf16[128,4,7168]{2,1,0:T(4,128)(2,1)}, u32[]{:S(2)}, u32[]{:S(2)}) %all-to-all-start) | async-done | bytes 7340064 | tf_op jit(solution)/shard_map/all_to_all | solution.py:240
  109.9 6.5 %return.1 = f32[128,128]{1,0:T(8,128)} custom-call(bf16[128,4,7168]{2,1,0:T(4,128)(2,1)} %all-to-all-done.rows_hbm, bf16[512,7168]{1,0:T(8,128)(2,1)} %project.1.project_hbm, f32[128,128]{1,0:T(8,128)S(1)} %get-tuple-element.5.weights_ref), custom_call_target="tpu_custom_call" | custom-call | flops 7340032 | bytes 14680064 | tf_op jit(solution)/shard_map/return/pallas_call | solution.py:267
  116.3 5.4 %all-to-all-start.1 = ((f32[128,1,128]{2,1,0:T(1,128)}), f32[128,1,128]{2,1,0:T(1,128)S(1)}, u32[]{:S(2)}, u32[]{:S(2)}) async-start(f32[128,1,128]{2,1,0:T(1,128)} %bitcast.2), calls=%async_computation.1 | async-start | bytes 131072 | tf_op jit(solution)/shard_map/all_to_all | solution.py:303
  121.7 12.3 %expert.1.raw_ref = f32[512,1024]{1,0:T(8,128)S(1)} custom-call(bf16[128,4,7168]{2,1,0:T(4,128)(2,1)} %all-to-all-done.rows_hbm, bf16[1,1024,7168]{2,1,0:T(8,128)(2,1)} %w_ref.1), custom_call_target="tpu_custom_call" | custom-call | flops 7516192768 | bytes 24117248 | tf_op jit(solution)/shard_map/expert/pallas_call | solution.py:284
  134.0 0.0 all-to-all-done.1
  134.0 1.9 %final.1 = (bf16[1,512,1024]{2,1,0:T(8,128)(2,1)}, f32[32,128]{1,0:T(8,128)}) custom-call(f32[512,1024]{1,0:T(8,128)S(1)} %expert.1.raw_ref, f32[128,128]{1,0:T(8,128)S(1)} %bitcast.5, f32[32,128]{1,0:T(8,128)S(1)} %get-tuple-element.6.rank_ref, f32[32,128]{1,0:T(8,128)S(1)} %get-tuple-element.7.chosen_ref), custom_call_target="tpu_custom_call" | custom-call | tf_op jit(solution)/shard_map/final/pallas_call | solution.py:306
Async XLA Ops:
  5.3 12.0 %copy-start = (s32[32,8]{0,1:T(8,128)S(1)}, s32[32,8]{0,1:T(8,128)}, u32[]{:S(2)}) copy-start(s32[32,8]{0,1:T(8,128)} %param.7) | copy-start | bytes 3076
  5.3 11.9 %copy-start.1 = (f32[32,128]{1,0:T(8,128)S(1)}, f32[32,128]{1,0:T(8,128)}, u32[]{:S(2)}) copy-start(f32[32,128]{1,0:T(8,128)} %logits_ref.1) | copy-start | bytes 49156
  5.3 12.6 %copy-start.2 = (bf16[1,512,1024]{2,1,0:T(8,128)(2,1)S(1)}, bf16[1,512,1024]{2,1,0:T(8,128)(2,1)}, u32[]{:S(2)}) copy-start(bf16[1,512,1024]{2,1,0:T(8,128)(2,1)} %hidden_ref.1) | copy-start | bytes 3145732
  5.3 104.6 %all-to-all-start = ((bf16[128,4,7168]{2,1,0:T(4,128)(2,1)}), bf16[128,4,7168]{2,1,0:T(4,128)(2,1)}, u32[]{:S(2)}, u32[]{:S(2)}) async-start(bf16[128,4,7168]{2,1,0:T(4,128)(2,1)} %pack.1), calls=%async_computation | async-start | bytes 14680064 | tf_op jit(solution)/shard_map/all_to_all | solution.py:240
  116.3 17.7 %all-to-all-start.1 = ((f32[128,1,128]{2,1,0:T(1,128)}), f32[128,1,128]{2,1,0:T(1,128)S(1)}, u32[]{:S(2)}, u32[]{:S(2)}) async-start(f32[128,1,128]{2,1,0:T(1,128)} %bitcast.2), calls=%async_computation.1 | async-start | bytes 131072 | tf_op jit(solution)/shard_map/all_to_all | solution.py:303

commit v4 on v3

--- a/solution.py
+++ b/solution.py
@@ -69,47 +69,60 @@
     out_ref[...] = out
 
 
-def project_kernel(hidden_ref, w_ref, out_ref):
-    out_ref[...] = jnp.dot(hidden_ref[...], w_ref[...], preferred_element_type=jnp.float32).astype(jnp.bfloat16)
-
-
-def return_kernel(rows_hbm, project_hbm, weights_ref, back_ref, rows, project, row_sems, project_sems):
+def project_kernel(hidden_ref, w_ref, held_ref, out_ref):
+    whole = jnp.dot(hidden_ref[...], w_ref[...], preferred_element_type=jnp.float32).astype(jnp.bfloat16)
+    held = held_ref.shape[0]
+    held_ref[...] = whole[:held]
+    out_ref[...] = whole[held:]
+
+
+def return_kernel(rows_hbm, kept_ref, project_hbm, weights_ref, back_ref, rows, project, row_sems, project_sems):
     blocks = row_sems.shape[0]
     slots, width = rows.shape[1:]
     peers = rows.shape[0] // blocks
+    held = blocks - project_sems.shape[0]
     lanes = back_ref.shape[1]
     part, wide = 8, 1024
 
-    def copies(b):
+    def row_copy(b):
         at = pl.ds(pl.multiple_of(b * peers, peers), peers)
-        to = pl.ds(pl.multiple_of(b * peers * slots, peers * slots), peers * slots)
-        return (
-            pltpu.make_async_copy(rows_hbm.at[at], rows.at[at], row_sems.at[b]),
-            pltpu.make_async_copy(project_hbm.at[to, :], project.at[to, :], project_sems.at[b]),
-        )
+        return pltpu.make_async_copy(rows_hbm.at[at], rows.at[at], row_sems.at[b])
+
+    def project_copy(b):
+        at = pl.ds(pl.multiple_of(b * peers * slots, peers * slots), peers * slots)
+        return pltpu.make_async_copy(project_hbm.at[at, :], project.at[at, :], project_sems.at[b])
 
     for b in range(blocks):
-        for copy in copies(b):
-            copy.start()
-
-    @pl.loop(0, blocks)
-    def _(b):
-        for copy in copies(b):
-            copy.wait()
+        row_copy(b).start()
+        if b >= held:
+            project_copy(b - held).start()
+
+    def block(b, source, first):
         for start in range(0, peers, part):
             at = pl.ds(pl.multiple_of(b * peers + start, part), part)
-            to = pl.ds(pl.multiple_of((b * peers + start) * slots, part * slots), part * slots)
+            to = pl.ds(pl.multiple_of(((b - first) * peers + start) * slots, part * slots), part * slots)
             total = jnp.zeros((part * slots, lanes), jnp.float32)
             for begin in range(0, width, wide):
                 columns = slice(begin, begin + wide)
                 row = rows[at, :, columns].reshape(part * slots, wide).astype(jnp.float32)
-                product = row * project[to, columns].astype(jnp.float32)
+                product = row * source[to, columns].astype(jnp.float32)
                 for column in range(0, wide, lanes):
                     total += product[:, column : column + lanes]
             grads = jnp.sum(total, 1, keepdims=True)
             slot = iota((part * slots, lanes), 0) % slots
             spread = jnp.where(slot == iota((part * slots, lanes), 1), grads, 0.0)
             back_ref[at, :] = weights_ref[at, :] + jnp.sum(spread.reshape(part, slots, lanes), 1)
+
+    @pl.loop(0, held)
+    def _(b):
+        row_copy(b).wait()
+        block(b, kept_ref, 0)
+
+    @pl.loop(held, blocks)
+    def _(b):
+        row_copy(b).wait()
+        project_copy(b - held).wait()
+        block(b, project, held)
 
 
 def expert_kernel(rows_hbm, w_hbm, raw_ref, arrived, rows, w, row_sems, w_sems):
@@ -249,15 +262,22 @@
         name="weights",
     )(routes_t, logits)
     span = 1024
-    project = pl.pallas_call(
+    held = capacity * 3 // 8
+    kept, project = pl.pallas_call(
         project_kernel,
         grid=(width // span,),
         in_specs=[
             pl.BlockSpec((None, capacity, units), lambda i: (0, 0, 0)),
             pl.BlockSpec((None, units, span), lambda i: (0, 0, i)),
         ],
-        out_specs=pl.BlockSpec((capacity, span), lambda i: (0, i)),
-        out_shape=pltpu.HBM((capacity, width), jnp.bfloat16),
+        out_specs=(
+            pl.BlockSpec((held, span), lambda i: (0, i)),
+            pl.BlockSpec((capacity - held, span), lambda i: (0, i)),
+        ),
+        out_shape=(
+            jax.ShapeDtypeStruct((held, width), jnp.bfloat16),
+            pltpu.HBM((capacity - held, width), jnp.bfloat16),
+        ),
         compiler_params=params(),
         cost_estimate=pl.CostEstimate(
             flops=2 * capacity * units * width, bytes_accessed=2 * units * width, transcendentals=0
@@ -266,21 +286,21 @@
     )(saved_hidden, in_hbm(w_down))
     back = pl.pallas_call(
         return_kernel,
-        in_specs=[far, far, near],
+        in_specs=[far, near, far, near],
         out_specs=near,
         out_shape=jax.ShapeDtypeStruct((experts, experts), jnp.float32),
         scratch_shapes=[
             pltpu.VMEM(packed, jnp.bfloat16),
-            pltpu.VMEM((capacity, width), jnp.bfloat16),
+            pltpu.VMEM((capacity - held, width), jnp.bfloat16),
             pltpu.SemaphoreType.DMA((8,)),
-            pltpu.SemaphoreType.DMA((8,)),
+            pltpu.SemaphoreType.DMA((5,)),
         ],
         compiler_params=params(),
         cost_estimate=pl.CostEstimate(
             flops=2 * capacity * width, bytes_accessed=4 * capacity * width, transcendentals=0
         ),
         name="return",
-    )(in_hbm(arrived), in_hbm(project), weights)
+    )(in_hbm(arrived), kept, in_hbm(project), weights)
     raw = pl.pallas_call(
         expert_kernel,
         in_specs=[far, far],

time: 136 us -> 136 us (level)
  transfers between devices with their start and end apart: 2 -> 2, of which waited for: 1 -> 1; matrix products, arithmetic and copies ran while one was open for 0% -> 0% of each run, Pallas kernels for 20% -> 19%
where the time goes in v4:
time: 136 us; the launch traced here: 135 us
  waiting for transfers between devices  77.6 us (57%)
  Pallas kernels  38.6 us (28%)
  starting transfers between devices  17.3 us (13%)
    all_to_all x1, waiting for transfers between devices, shards(): lax.all_to_all(sent, ('node', 'expert'), split_axis=0, concat_axis=0, til...  77.6 us
    pallas_call x1, Pallas kernels, shards(): pl.pallas_call(project_kernel, grid=(width // span,), in_specs=[pl.BlockS...  13.1 us
    pallas_call x1, Pallas kernels, shards(): pl.pallas_call(expert_kernel, in_specs=[far, far], out_shape=jax.ShapeDty...  12.3 us
    all_to_all x1, starting transfers between devices, shards(): lax.all_to_all(sent, ('node', 'expert'), split_axis=0, concat_axis=0, til...  11.9 us
    pallas_call x1, Pallas kernels, shards(): pl.pallas_call(return_kernel, in_specs=[far, near, far, near], out_specs=...  6.02 us
    all_to_all x1, starting transfers between devices, shards(): lax.all_to_all(back.reshape(experts, 1, experts), ('node', 'expert'), spl...  5.37 us
    pallas_call x1, Pallas kernels, shards(): pl.pallas_call(functools.partial(pack_kernel, slots), in_specs=[near, nea...  4.67 us
  transfers between devices with their start and end apart: 2, of which 1 were waited for; matrix products, arithmetic and copies ran while one was open for 0% of the time, Pallas kernels for 19%

profile of v4, /device:TPU:1, one launch (start us, length us, event | category | flops | bytes accessed | tf_op | source)
XLA Modules:
  0.0 135.4 jit_solution(4730516324079653718)
XLA Ops:
  0.6 4.7 %pack.1 = bf16[128,4,7168]{2,1,0:T(4,128)(2,1)} custom-call(s32[8,32]{1,0:T(8,128)} %bitcast.6, bf16[32,7168]{1,0:T(8,128)(2,1)} %grad_ref.1), custom_call_target="tpu_custom_call" | custom-call | flops 234881024 | bytes 7340032 | tf_op jit(solution)/shard_map/pack/pallas_call | solution.py:241
  5.3 0.0 copy-start
  5.3 0.0 copy-start.1
  5.3 11.9 %all-to-all-start = ((bf16[128,4,7168]{2,1,0:T(4,128)(2,1)}), bf16[128,4,7168]{2,1,0:T(4,128)(2,1)}, u32[]{:S(2)}, u32[]{:S(2)}) async-start(bf16[128,4,7168]{2,1,0:T(4,128)(2,1)} %pack.1), calls=%async_computation | async-start | bytes 14680064 | tf_op jit(solution)/shard_map/all_to_all | solution.py:253
  17.2 0.0 copy-done
  17.3 0.0 copy-done.1
  17.3 0.6 weights.1
  17.9 0.0 copy-start.2
  17.9 1.2 copy-done.2
  19.1 13.1 %project.1 = (bf16[192,7168]{1,0:T(8,128)(2,1)S(1)}, bf16[320,7168]{1,0:T(8,128)(2,1)}) custom-call(bf16[1,512,1024]{2,1,0:T(8,128)(2,1)S(1)} %copy-done.2, bf16[1,1024,7168]{2,1,0:T(8,128)(2,1)} %w_ref.1), custom_call_target="tpu_custom_call" | custom-call | flops 7516192768 | bytes 14680064 | tf_op jit(solution)/shard_map/project/pallas_call | solution.py:266
  32.2 77.6 %all-to-all-done.rows_hbm = bf16[128,4,7168]{2,1,0:T(4,128)(2,1)} async-done(((bf16[128,4,7168]{2,1,0:T(4,128)(2,1)}), bf16[128,4,7168]{2,1,0:T(4,128)(2,1)}, u32[]{:S(2)}, u32[]{:S(2)}) %all-to-all-start) | async-done | bytes 7340064 | tf_op jit(solution)/shard_map/all_to_all | solution.py:253
  109.9 6.0 %return.1 = f32[128,128]{1,0:T(8,128)} custom-call(bf16[128,4,7168]{2,1,0:T(4,128)(2,1)} %all-to-all-done.rows_hbm, bf16[192,7168]{1,0:T(8,128)(2,1)S(1)} %get-tuple-element.7.kept_ref, bf16[320,7168]{1,0:T(8,128)(2,1)} %get-tuple-element.8.project_hbm, f32[128,128]{1,0:T(8,128)S(1)} %get-tuple-element.9.weights_ref), custom_call_target="tpu_custom_call" | custom-call | flops 7340032 | bytes 14680064 | tf_op jit(solution)/shard_map/return/pallas_call | solution.py:287
  115.9 5.4 %all-to-all-start.1 = ((f32[128,1,128]{2,1,0:T(1,128)}), f32[128,1,128]{2,1,0:T(1,128)S(1)}, u32[]{:S(2)}, u32[]{:S(2)}) async-start(f32[128,1,128]{2,1,0:T(1,128)} %bitcast.2), calls=%async_computation.1 | async-start | bytes 131072 | tf_op jit(solution)/shard_map/all_to_all | solution.py:323
  121.3 12.3 %expert.1.raw_ref = f32[512,1024]{1,0:T(8,128)S(1)} custom-call(bf16[128,4,7168]{2,1,0:T(4,128)(2,1)} %all-to-all-done.rows_hbm, bf16[1,1024,7168]{2,1,0:T(8,128)(2,1)} %w_ref.1), custom_call_target="tpu_custom_call" | custom-call | flops 7516192768 | bytes 24117248 | tf_op jit(solution)/shard_map/expert/pallas_call | solution.py:304
  133.6 0.0 all-to-all-done.1
  133.6 1.9 %final.1 = (bf16[1,512,1024]{2,1,0:T(8,128)(2,1)}, f32[32,128]{1,0:T(8,128)}) custom-call(f32[512,1024]{1,0:T(8,128)S(1)} %expert.1.raw_ref, f32[128,128]{1,0:T(8,128)S(1)} %bitcast.5, f32[32,128]{1,0:T(8,128)S(1)} %get-tuple-element.10.rank_ref, f32[32,128]{1,0:T(8,128)S(1)} %get-tuple-element.11.chosen_ref), custom_call_target="tpu_custom_call" | custom-call | tf_op jit(solution)/shard_map/final/pallas_call | solution.py:326
Async XLA Ops:
  5.3 11.9 %copy-start = (s32[32,8]{0,1:T(8,128)S(1)}, s32[32,8]{0,1:T(8,128)}, u32[]{:S(2)}) copy-start(s32[32,8]{0,1:T(8,128)} %param.7) | copy-start | bytes 3076
  5.3 11.9 %copy-start.1 = (f32[32,128]{1,0:T(8,128)S(1)}, f32[32,128]{1,0:T(8,128)}, u32[]{:S(2)}) copy-start(f32[32,128]{1,0:T(8,128)} %logits_ref.1) | copy-start | bytes 49156
  5.3 104.6 %all-to-all-start = ((bf16[128,4,7168]{2,1,0:T(4,128)(2,1)}), bf16[128,4,7168]{2,1,0:T(4,128)(2,1)}, u32[]{:S(2)}, u32[]{:S(2)}) async-start(bf16[128,4,7168]{2,1,0:T(4,128)(2,1)} %pack.1), calls=%async_computation | async-start | bytes 14680064 | tf_op jit(solution)/shard_map/all_to_all | solution.py:253
  17.9 1.2 copy-start.2
  115.9 17.7 %all-to-all-start.1 = ((f32[128,1,128]{2,1,0:T(1,128)}), f32[128,1,128]{2,1,0:T(1,128)S(1)}, u32[]{:S(2)}, u32[]{:S(2)}) async-start(f32[128,1,128]{2,1,0:T(1,128)} %bitcast.2), calls=%async_computation.1 | async-start | bytes 131072 | tf_op jit(solution)/shard_map/all_to_all | solution.py:323

commit v5 on v4

--- a/solution.py
+++ b/solution.py
@@ -82,7 +82,7 @@
     peers = rows.shape[0] // blocks
     held = blocks - project_sems.shape[0]
     lanes = back_ref.shape[1]
-    part, wide = 8, 1024
+    part, wide = 16, 512
 
     def row_copy(b):
         at = pl.ds(pl.multiple_of(b * peers, peers), peers)
@@ -333,7 +333,7 @@
         ),
         scratch_shapes=[
             pltpu.VMEM((capacity, units), jnp.bfloat16),
-            pltpu.SemaphoreType.DMA((4,)),
+            pltpu.SemaphoreType.DMA((8,)),
         ],
         compiler_params=params(),
         name="final",

time: 136 us -> 136 us (level)
  no operation moved by 1% of the time
where the time goes in v5:
time: 136 us; the launch traced here: 135 us
  waiting for transfers between devices  77.6 us (57%)
  Pallas kernels  38.6 us (28%)
  starting transfers between devices  17.3 us (13%)
    all_to_all x1, waiting for transfers between devices, shards(): lax.all_to_all(sent, ('node', 'expert'), split_axis=0, concat_axis=0, til...  77.6 us
    pallas_call x1, Pallas kernels, shards(): pl.pallas_call(project_kernel, grid=(width // span,), in_specs=[pl.BlockS...  13.1 us
    pallas_call x1, Pallas kernels, shards(): pl.pallas_call(expert_kernel, in_specs=[far, far], out_shape=jax.ShapeDty...  12.3 us
    all_to_all x1, starting transfers between devices, shards(): lax.all_to_all(sent, ('node', 'expert'), split_axis=0, concat_axis=0, til...  11.9 us
    pallas_call x1, Pallas kernels, shards(): pl.pallas_call(return_kernel, in_specs=[far, near, far, near], out_specs=...  6 us
    all_to_all x1, starting transfers between devices, shards(): lax.all_to_all(back.reshape(experts, 1, experts), ('node', 'expert'), spl...  5.37 us
    pallas_call x1, Pallas kernels, shards(): pl.pallas_call(functools.partial(pack_kernel, slots), in_specs=[near, nea...  4.67 us
  transfers between devices with their start and end apart: 2, of which 1 were waited for; matrix products, arithmetic and copies ran while one was open for 0% of the time, Pallas kernels for 19%

profile of v5, /device:TPU:1, one launch (start us, length us, event | category | flops | bytes accessed | tf_op | source)
XLA Modules:
  0.0 135.4 jit_solution(11075886000681610164)
XLA Ops:
  0.6 4.7 %pack.1 = bf16[128,4,7168]{2,1,0:T(4,128)(2,1)} custom-call(s32[8,32]{1,0:T(8,128)} %bitcast.6, bf16[32,7168]{1,0:T(8,128)(2,1)} %grad_ref.1), custom_call_target="tpu_custom_call" | custom-call | flops 234881024 | bytes 7340032 | tf_op jit(solution)/shard_map/pack/pallas_call | solution.py:241
  5.3 0.0 copy-start
  5.3 0.0 copy-start.1
  5.3 11.9 %all-to-all-start = ((bf16[128,4,7168]{2,1,0:T(4,128)(2,1)}), bf16[128,4,7168]{2,1,0:T(4,128)(2,1)}, u32[]{:S(2)}, u32[]{:S(2)}) async-start(bf16[128,4,7168]{2,1,0:T(4,128)(2,1)} %pack.1), calls=%async_computation | async-start | bytes 14680064 | tf_op jit(solution)/shard_map/all_to_all | solution.py:253
  17.2 0.0 copy-done
  17.3 0.0 copy-done.1
  17.3 0.6 weights.1
  17.9 0.0 copy-start.2
  17.9 1.2 copy-done.2
  19.1 13.1 %project.1 = (bf16[192,7168]{1,0:T(8,128)(2,1)S(1)}, bf16[320,7168]{1,0:T(8,128)(2,1)}) custom-call(bf16[1,512,1024]{2,1,0:T(8,128)(2,1)S(1)} %copy-done.2, bf16[1,1024,7168]{2,1,0:T(8,128)(2,1)} %w_ref.1), custom_call_target="tpu_custom_call" | custom-call | flops 7516192768 | bytes 14680064 | tf_op jit(solution)/shard_map/project/pallas_call | solution.py:266
  32.2 77.6 %all-to-all-done.rows_hbm = bf16[128,4,7168]{2,1,0:T(4,128)(2,1)} async-done(((bf16[128,4,7168]{2,1,0:T(4,128)(2,1)}), bf16[128,4,7168]{2,1,0:T(4,128)(2,1)}, u32[]{:S(2)}, u32[]{:S(2)}) %all-to-all-start) | async-done | bytes 7340064 | tf_op jit(solution)/shard_map/all_to_all | solution.py:253
  109.9 6.0 %return.1 = f32[128,128]{1,0:T(8,128)} custom-call(bf16[128,4,7168]{2,1,0:T(4,128)(2,1)} %all-to-all-done.rows_hbm, bf16[192,7168]{1,0:T(8,128)(2,1)S(1)} %get-tuple-element.7.kept_ref, bf16[320,7168]{1,0:T(8,128)(2,1)} %get-tuple-element.8.project_hbm, f32[128,128]{1,0:T(8,128)S(1)} %get-tuple-element.9.weights_ref), custom_call_target="tpu_custom_call" | custom-call | flops 7340032 | bytes 14680064 | tf_op jit(solution)/shard_map/return/pallas_call | solution.py:287
  115.9 5.4 %all-to-all-start.1 = ((f32[128,1,128]{2,1,0:T(1,128)}), f32[128,1,128]{2,1,0:T(1,128)S(1)}, u32[]{:S(2)}, u32[]{:S(2)}) async-start(f32[128,1,128]{2,1,0:T(1,128)} %bitcast.2), calls=%async_computation.1 | async-start | bytes 131072 | tf_op jit(solution)/shard_map/all_to_all | solution.py:323
  121.3 12.3 %expert.1.raw_ref = f32[512,1024]{1,0:T(8,128)S(1)} custom-call(bf16[128,4,7168]{2,1,0:T(4,128)(2,1)} %all-to-all-done.rows_hbm, bf16[1,1024,7168]{2,1,0:T(8,128)(2,1)} %w_ref.1), custom_call_target="tpu_custom_call" | custom-call | flops 7516192768 | bytes 24117248 | tf_op jit(solution)/shard_map/expert/pallas_call | solution.py:304
  133.6 0.0 all-to-all-done.1
  133.6 1.9 %final.1 = (bf16[1,512,1024]{2,1,0:T(8,128)(2,1)}, f32[32,128]{1,0:T(8,128)}) custom-call(f32[512,1024]{1,0:T(8,128)S(1)} %expert.1.raw_ref, f32[128,128]{1,0:T(8,128)S(1)} %bitcast.5, f32[32,128]{1,0:T(8,128)S(1)} %get-tuple-element.10.rank_ref, f32[32,128]{1,0:T(8,128)S(1)} %get-tuple-element.11.chosen_ref), custom_call_target="tpu_custom_call" | custom-call | tf_op jit(solution)/shard_map/final/pallas_call | solution.py:326
Async XLA Ops:
  5.3 11.9 %copy-start = (s32[32,8]{0,1:T(8,128)S(1)}, s32[32,8]{0,1:T(8,128)}, u32[]{:S(2)}) copy-start(s32[32,8]{0,1:T(8,128)} %param.7) | copy-start | bytes 3076
  5.3 11.9 %copy-start.1 = (f32[32,128]{1,0:T(8,128)S(1)}, f32[32,128]{1,0:T(8,128)}, u32[]{:S(2)}) copy-start(f32[32,128]{1,0:T(8,128)} %logits_ref.1) | copy-start | bytes 49156
  5.3 104.6 %all-to-all-start = ((bf16[128,4,7168]{2,1,0:T(4,128)(2,1)}), bf16[128,4,7168]{2,1,0:T(4,128)(2,1)}, u32[]{:S(2)}, u32[]{:S(2)}) async-start(bf16[128,4,7168]{2,1,0:T(4,128)(2,1)} %pack.1), calls=%async_computation | async-start | bytes 14680064 | tf_op jit(solution)/shard_map/all_to_all | solution.py:253
  17.9 1.2 copy-start.2
  115.9 17.7 %all-to-all-start.1 = ((f32[128,1,128]{2,1,0:T(1,128)}), f32[128,1,128]{2,1,0:T(1,128)S(1)}, u32[]{:S(2)}, u32[]{:S(2)}) async-start(f32[128,1,128]{2,1,0:T(1,128)} %bitcast.2), calls=%async_computation.1 | async-start | bytes 131072 | tf_op jit(solution)/shard_map/all_to_all | solution.py:323
